TPU v7x, 32 devices: a whole 2x2x4 slice. The times are simulated.
32 devices in a mesh: node: 4 (over y, x), grid: 8 (over z, core).
Axes of the slice: x: 2, y: 2, z: 4, core: 2. Of those that a mesh axis runs over, the one named last changes fastest.
Arguments:
- probes: float32 [1, 48, 192, 256], P(None, 'grid'), may hold values from -6 to 6
- potential: float32 [48, 192, 256], P('grid'), may hold values from -2 to 1
- warm_start: bfloat16 [4, 1, 2, 48, 192, 256], P('node', None, None, 'grid'), may hold values from -0.29882812 to 0.29882812
- shift_points: float32 [4, 2], P('node'), may hold values from -4 to 9, as said below
- quad_weights: float32 [4, 2], P('node'), may hold values from -0.3 to 0.3
Outputs:
- moments: float32 [2, 1, 2, 48, 192, 256], P(None, None, None, 'grid', 'node')
- trace_estimate: float32 [2], replicated
Inputs may be any that keep to these rules, and one draw needn't show every extreme that they name: `shift_points`: column 0 holds real parts in -1 to 9; column 1 holds imaginary parts whose magnitude lies in 1 to 4.
All inputs are finite; a program needn't handle non-finite values.
Results may differ from a plain program's by a relative error of at most 0.0003.
Values may be sent and summed in bfloat16 or wider, within the bound.
A program may use at most 192 MiB of HBM per device.

v0:
```python
import functools

import jax
import jax.numpy as jnp
import ml_dtypes
import numpy as np
from jax import lax
from jax.experimental import pallas as pl
from jax.experimental.pallas import tpu as pltpu
from jax.sharding import PartitionSpec as P

MESH = pl.DeviceIdType.MESH
SUMS = 16
CHUNK = 32


def ring_matrix(size, diagonal):
    matrix = np.zeros((size, size), np.float32)
    at = np.arange(size)
    for step, weight in ((1, 16.0), (2, -1.0)):
        matrix[at, (at + step) % size] += weight
        matrix[at, (at - step) % size] += weight
    matrix[at, at] += diagonal
    return matrix.astype(ml_dtypes.bfloat16)


def cmul(a, b):
    return a[0] * b[0] - a[1] * b[1], a[0] * b[1] + a[1] * b[0]


def cdiv(a, b):
    size = b[0] * b[0] + b[1] * b[1]
    return (a[0] * b[0] + a[1] * b[1]) / size, (a[1] * b[0] - a[0] * b[1]) / size


def fold(values):
    rows, cols = values.shape
    return jnp.sum(values.reshape(rows // 8, 8, cols), axis=0)


def kernel(
    nodes,
    slabs,
    warm,
    probes,
    potential,
    shift_hbm,
    weight_hbm,
    along_x_hbm,
    along_y_hbm,
    moments,
    trace,
    xbuf,
    bbuf,
    vbuf,
    rbuf,
    qbuf,
    plane,
    acc,
    sums,
    far_out,
    far_in,
    edge_out,
    edge_in,
    xwide,
    peer_x,
    peer_r,
    peer_q,
    late,
    peer_late,
    notes,
    shift_ref,
    weight_ref,
    along_x,
    along_y,
    local_sem,
    x_send,
    x_recv,
    r_send,
    r_recv,
    q_send,
    q_recv,
    s_send,
    s_recv,
    n_send,
    n_recv,
    g_send,
    g_recv,
    e_send,
    e_recv,
):
    node, slab = lax.axis_index("node"), lax.axis_index("grid")
    depth, width, length = bbuf.shape
    half = width // 2
    block = width // nodes
    above = (node, lax.rem(slab + 1, slabs))
    below = (node, lax.rem(slab + slabs - 1, slabs))

    loads = [
        pltpu.make_async_copy(warm.at[0, 0], xbuf.at[:, 2 : depth + 2], local_sem.at[0]),
        pltpu.make_async_copy(probes.at[0], bbuf, local_sem.at[1]),
        pltpu.make_async_copy(potential, vbuf, local_sem.at[2]),
        pltpu.make_async_copy(shift_hbm, shift_ref, local_sem.at[3]),
        pltpu.make_async_copy(weight_hbm, weight_ref, local_sem.at[4]),
        pltpu.make_async_copy(along_x_hbm, along_x, local_sem.at[5]),
        pltpu.make_async_copy(along_y_hbm, along_y, local_sem.at[6]),
    ]
    for load in loads:
        load.start()

    barrier = pltpu.get_barrier_semaphore()
    for k in range(1, slabs):
        pl.semaphore_signal(
            barrier, inc=1, device_id=(node, lax.rem(slab + k, slabs)), device_id_type=MESH
        )
    for k in range(1, nodes):
        pl.semaphore_signal(
            barrier, inc=1, device_id=(lax.rem(node + k, nodes), slab), device_id_type=MESH
        )
    pl.semaphore_wait(barrier, slabs + nodes - 2)

    def send(source, target, send_sem, recv_sem, device):
        copy = pltpu.make_async_remote_copy(
            src_ref=source,
            dst_ref=target,
            send_sem=send_sem,
            recv_sem=recv_sem,
            device_id=device,
            device_id_type=MESH,
        )
        copy.start()
        return copy

    x_down = send(
        warm.at[0, 0, :, 0:2], xbuf.at[:, depth + 2 : depth + 4], x_send.at[0], x_recv.at[0], below
    )
    x_up = send(warm.at[0, 0, :, depth - 2 : depth], xbuf.at[:, 0:2], x_send.at[1], x_recv.at[1], above)

    groups = ((2, depth - 3), (0, 2))
    early = {}

    def share_rows(kind, source, target, offset, group):
        first, last = groups[group]
        slot = 2 * kind + group
        step = 16 if block % 16 == 0 else 8
        copies = []
        for k in range(1, nodes):
            peer = lax.rem(node + k, nodes)
            rows = pl.ds(pl.multiple_of(peer * block, step), block)
            copies.append(
                send(
                    source.at[:, first + offset : last + offset, rows, :],
                    target.at[k, :, first:last],
                    e_send.at[k, slot],
                    e_recv.at[k, slot],
                    (peer, slab),
                )
            )
        early[kind, group] = copies

    narrow = block % 16 == 0
    if narrow:
        for group in range(2):
            share_rows(0, warm.at[0, 0], peer_x, 0, group)

    acc[...] = jnp.zeros_like(acc)
    qbuf[:, depth : depth + 2, half:, :] = jnp.zeros((2, 2, width - half, length), jnp.float32)
    for load in loads:
        load.wait()
    shift = shift_ref[0, 0], shift_ref[0, 1]

    def dot(a, b):
        return jnp.dot(a, b, preferred_element_type=jnp.float32)

    def in_plane_exact(p):
        for part in range(2):
            field = xbuf[part, p + 2]
            plane[part] = dot(field, along_y[...]) + dot(along_x[...], field)

    def in_plane(source, p):
        for part in range(2):
            field = source[part, p]
            high = field.astype(jnp.bfloat16)
            low = (field - high.astype(jnp.float32)).astype(jnp.bfloat16)
            plane[part] = (dot(high, along_y[...]) + dot(low, along_y[...])) + (
                dot(along_x[...], high) + dot(along_x[...], low)
            )

    def apply(field, stencil, local):
        diagonal = shift[0] - local
        return (
            diagonal * field[0] - shift[1] * field[1] + stencil[0] * (1.0 / 24.0),
            diagonal * field[1] + shift[1] * field[0] + stencil[1] * (1.0 / 24.0),
        )

    def in_chunks(first, terms):
        count = terms[1]

        def step(i, totals):
            rows = pl.ds(pl.multiple_of(i * CHUNK, CHUNK), CHUNK)
            values = terms[0](rows)
            return tuple(total + fold(value) for total, value in zip(totals, values))

        zero = jnp.zeros((8, length), jnp.float32)
        totals = lax.fori_loop(0, width // CHUNK, step, (zero,) * count)
        for i, total in enumerate(totals):
            acc[first + i] += total

    def residual_plane(p, carry):
        in_plane_exact(p)

        def terms(rows):
            stencil, field = [], []
            for part in range(2):
                at = [xbuf[part, p + j, rows, :].astype(jnp.float32) for j in range(5)]
                stencil.append(plane[part, rows, :] + 16.0 * (at[1] + at[3]) - (at[0] + at[4]))
                field.append(at[2])
            source = bbuf[p, rows, :]
            image = apply(field, stencil, vbuf[p, rows, :])
            r = source - image[0], -image[1]
            if not narrow:
                for part in range(2):
                    xwide[part, p, rows, :] = field[part]
            rbuf[0, p + 2, rows, :] = r[0]
            rbuf[1, p + 2, rows, :] = r[1]
            return (
                r[0] * r[0] - r[1] * r[1],
                2.0 * r[0] * r[1],
                source * field[0],
                source * field[1],
                source * r[0],
                source * r[1],
            )

        in_chunks(0, (terms, 6))
        return carry

    def image_plane(p, carry):
        in_plane(rbuf, p + 2)

        def terms(rows):
            stencil, field = [], []
            for part in range(2):
                at = [rbuf[part, p + j, rows, :] for j in range(5)]
                stencil.append(plane[part, rows, :] + 16.0 * (at[1] + at[3]) - (at[0] + at[4]))
                field.append(at[2])
            source = bbuf[p, rows, :]
            q = apply(field, stencil, vbuf[p, rows, :])
            qbuf[0, p, rows, :] = q[0]
            qbuf[1, p, rows, :] = q[1]
            return (
                *cmul(field, q),
                q[0] * q[0] - q[1] * q[1],
                2.0 * q[0] * q[1],
                source * q[0],
                source * q[1],
            )

        in_chunks(6, (terms, 6))
        return carry

    def energy_plane(p, carry):
        in_plane(qbuf, p)

        def terms(rows):
            stencil, field = [], []
            for part in range(2):
                stencil.append(
                    plane[part, rows, :]
                    + 32.0 * qbuf[part, p + 1, rows, :]
                    - 2.0 * qbuf[part, p + 2, rows, :]
                )
                field.append(qbuf[part, p, rows, :])
            return cmul(field, apply(field, stencil, vbuf[p, rows, :]))

        in_chunks(12, (terms, 2))
        return carry

    def narrowed(source, target):
        target[...] = source[...].astype(jnp.bfloat16)

    def widened(source, target):
        target[...] = source[...].astype(jnp.float32)

    def shared(group):
        if not narrow:
            share_rows(0, xwide, peer_x, 0, group)
        share_rows(1, rbuf, peer_r, 2, group)

    with jax.named_scope("residual"):
        lax.fori_loop(2, depth - 2, residual_plane, 0)
        shared(0)
        x_up.wait_recv()
        x_down.wait_recv()
        lax.fori_loop(0, 2, residual_plane, 0)
        near_down = send(
            rbuf.at[:, 2], rbuf.at[:, depth + 2], r_send.at[0], r_recv.at[0], below
        )
        narrowed(rbuf.at[:, 3], far_out.at[0])
        far_down = send(far_out.at[0], far_in.at[0], g_send.at[0], g_recv.at[0], below)
        lax.fori_loop(depth - 2, depth, residual_plane, 0)
        near_up = send(rbuf.at[:, depth + 1], rbuf.at[:, 1], r_send.at[1], r_recv.at[1], above)
        narrowed(rbuf.at[:, depth], far_out.at[1])
        far_up = send(far_out.at[1], far_in.at[1], g_send.at[1], g_recv.at[1], above)
        shared(1)

    with jax.named_scope("image"):
        lax.fori_loop(2, depth - 2, image_plane, 0)
        share_rows(2, qbuf, peer_q, 0, 0)
        near_up.wait_recv()
        far_up.wait_recv()
        widened(far_in.at[1], rbuf.at[:, 0])
        lax.fori_loop(0, 2, image_plane, 0)
        narrowed(qbuf.at[:, 0:2, 0:half], edge_out.at[0])
        q_down = send(edge_out.at[0], edge_in.at[0], q_send.at[0], q_recv.at[0], below)
        near_down.wait_recv()
        far_down.wait_recv()
        widened(far_in.at[0], rbuf.at[:, depth + 3])
        lax.fori_loop(depth - 2, depth, image_plane, 0)
        narrowed(qbuf.at[:, depth - 2 : depth, half:width], edge_out.at[1])
        q_up = send(edge_out.at[1], edge_in.at[1], q_send.at[1], q_recv.at[1], above)
        share_rows(2, qbuf, peer_q, 0, 1)

    with jax.named_scope("energy"):
        lax.fori_loop(0, depth - 2, energy_plane, 0)
        q_down.wait_recv()
        widened(edge_in.at[0], qbuf.at[:, depth : depth + 2, 0:half])
        lax.fori_loop(depth - 2, depth, energy_plane, 0)
        q_up.wait_recv()

        def crossing(i, totals):
            start = i * CHUNK
            mine = pl.ds(pl.multiple_of(half + start, CHUNK), CHUNK)
            theirs = pl.ds(pl.multiple_of(start, CHUNK), CHUNK)
            near = [edge_in[1, part, 1, theirs, :].astype(jnp.float32) for part in range(2)]
            far = [edge_in[1, part, 0, theirs, :].astype(jnp.float32) for part in range(2)]
            zeroth = [qbuf[part, 0, mine, :] for part in range(2)]
            first = [qbuf[part, 1, mine, :] for part in range(2)]
            one = cmul(zeroth, [32.0 * near[part] - 2.0 * far[part] for part in range(2)])
            two = cmul(first, near)
            return tuple(
                totals[part] + fold((one[part] - 2.0 * two[part]) * (1.0 / 24.0)) for part in range(2)
            )

        zero = jnp.zeros((8, length), jnp.float32)
        totals = lax.fori_loop(0, half // CHUNK, crossing, (zero, zero))
        acc[12] += totals[0]
        acc[13] += totals[1]

    with jax.named_scope("scalars"):
        partial = jnp.sum(acc[...], axis=1)
        lanes = partial[:, 0:128]
        for at in range(128, length, 128):
            lanes = lanes + partial[:, at : at + 128]
        sums[0] = lanes
        scalar_copies = [
            send(
                sums.at[0],
                sums.at[k],
                s_send.at[k],
                s_recv.at[k],
                (node, lax.rem(slab + k, slabs)),
            )
            for k in range(1, slabs)
        ]
        for copy in scalar_copies:
            copy.wait_recv()
        total = jnp.zeros((SUMS, 128), jnp.float32)
        for owner in range(slabs):
            total = total + sums[lax.rem(slab - owner + slabs, slabs)]
        total = jnp.broadcast_to(jnp.sum(total, axis=1, keepdims=True), (SUMS, length))
        pair = lambda i: (total[i : i + 1], total[i + 1 : i + 2])
        s0, t0, t1, s1, s2, t2, s3 = (pair(i) for i in range(0, 14, 2))
        step0 = cdiv(s0, s1)
        square = cmul(step0, step0)
        norm1 = cmul(square, s2)
        norm1 = norm1[0] - s0[0], norm1[1] - s0[1]
        ratio = cdiv(norm1, s0)
        grow = ratio[0] + 1.0, ratio[1]
        one = cmul(cmul(grow, grow), s1)
        two = cmul(cmul(grow, step0), s2)
        three = cmul(square, s3)
        step1 = cdiv(
            norm1, (one[0] - 2.0 * two[0] + three[0], one[1] - 2.0 * two[1] + three[1])
        )
        coef_r = cmul(step1, grow)
        coef_r = coef_r[0] + step0[0], coef_r[1] + step0[1]
        coef_q = cmul(step1, step0)
        coef_q = -coef_q[0], -coef_q[1]
        inner_r, inner_q = cmul(coef_r, t1), cmul(coef_q, t2)
        inner = t0[0] + inner_r[0] + inner_q[0], t0[1] + inner_r[1] + inner_q[1]
        weight = weight_ref[0, 0], weight_ref[0, 1]
        share = cmul(weight, inner)
        following = cmul(weight, ((shift[0] - 4.0) * 0.2, shift[1] * 0.2))
        row = lax.broadcasted_iota(jnp.int32, (16, 128), 0)
        note = jnp.zeros((16, 128), jnp.float32)
        entries = (*weight, *following, *(v[:, 0:128] for v in (*share, *coef_r, *coef_q)))
        for i, entry in enumerate(entries):
            note = jnp.where(row == i, entry, note)
        notes[0] = note
        note_copies = [
            send(notes.at[0], notes.at[k], n_send.at[k], n_recv.at[k], (lax.rem(node + k, nodes), slab))
            for k in range(1, nodes)
        ]

    with jax.named_scope("moments"):
        late_first = depth - 3
        late_copies = []

        def late_plane(p):
            def step(i, carry):
                rows = pl.ds(pl.multiple_of(i * CHUNK, CHUNK), CHUNK)
                r = rbuf[0, p + 2, rows, :], rbuf[1, p + 2, rows, :]
                q = qbuf[0, p, rows, :], qbuf[1, p, rows, :]
                along_r, along_q = cmul(coef_r, r), cmul(coef_q, q)
                for part in range(2):
                    start = xbuf[part, p + 2, rows, :].astype(jnp.float32)
                    late[p - late_first, part, rows, :] = start + along_r[part] + along_q[part]
                return carry

            lax.fori_loop(0, width // CHUNK, step, 0)

        for p in range(late_first, depth):
            late_plane(p)
            for k in range(1, nodes):
                peer = lax.rem(node + k, nodes)
                late_copies.append(
                    send(
                        late.at[p - late_first, :, pl.ds(pl.multiple_of(peer * block, 8), block), :],
                        peer_late.at[k, p - late_first],
                        e_send.at[k, 6 + p - late_first],
                        e_recv.at[k, 6 + p - late_first],
                        (peer, slab),
                    )
                )

        for copy in note_copies:
            copy.wait_recv()
        whole_trace = jnp.zeros((16, 128), jnp.float32)
        for owner in range(nodes):
            whole_trace = whole_trace + notes[lax.rem(node - owner + nodes, nodes)]
        lane = lax.broadcasted_iota(jnp.int32, (16, 128), 1)
        for part in range(2):
            trace[part] = jnp.sum(jnp.where((row == 4 + part) & (lane == 0), whole_trace, 0.0))
        factors = []
        for k in range(nodes):
            first_lane = jnp.where(lane == 0, notes[k], 0.0)
            wide = jnp.broadcast_to(jnp.sum(first_lane, axis=1, keepdims=True), (16, length))
            factors.append([(wide[i : i + 1], wide[i + 1 : i + 2]) for i in (0, 2, 6, 8)])
        piece = 16 if narrow else 8

        def late_moment_plane(at, carry):
            def step(i, inner_carry):
                there = pl.ds(pl.multiple_of(i * piece, piece), piece)
                here = pl.ds(pl.multiple_of(node * block + i * piece, piece), piece)
                values = [None] * 4
                for k in range(nodes):
                    if k:
                        field = [peer_late[k, at, part, there, :] for part in range(2)]
                    else:
                        field = [late[at, part, here, :] for part in range(2)]
                    for degree in range(2):
                        term = cmul(factors[k][degree], field)
                        for part in range(2):
                            n = 2 * degree + part
                            values[n] = term[part] if k == 0 else values[n] + term[part]
                for degree in range(2):
                    for part in range(2):
                        moments[degree, 0, part, late_first + at, there, :] = values[2 * degree + part]
                return inner_carry

            lax.fori_loop(0, block // piece, step, 0)
            return carry

        def moment_plane(p, carry):
            def step(i, inner_carry):
                there = pl.ds(pl.multiple_of(i * piece, piece), piece)
                here = pl.ds(pl.multiple_of(node * block + i * piece, piece), piece)
                values = [None] * 4
                for k in range(nodes):
                    if k:
                        x, r, q = (
                            [ref[k, part, p, there, :] for part in range(2)]
                            for ref in (peer_x, peer_r, peer_q)
                        )
                    else:
                        if narrow:
                            x = [xbuf[part, p + 2, here, :] for part in range(2)]
                        else:
                            x = [xwide[part, p, here, :] for part in range(2)]
                        r = [rbuf[part, p + 2, here, :] for part in range(2)]
                        q = [qbuf[part, p, here, :] for part in range(2)]
                    along_r, along_q = cmul(factors[k][2], r), cmul(factors[k][3], q)
                    field = [
                        x[part].astype(jnp.float32) + along_r[part] + along_q[part]
                        for part in range(2)
                    ]
                    for degree in range(2):
                        term = cmul(factors[k][degree], field)
                        for part in range(2):
                            at = 2 * degree + part
                            values[at] = term[part] if k == 0 else values[at] + term[part]
                for degree in range(2):
                    for part in range(2):
                        moments[degree, 0, part, p, there, :] = values[2 * degree + part]
                return inner_carry

            lax.fori_loop(0, block // piece, step, 0)
            return carry

        for group, (first, last) in enumerate(groups):
            for kind in range(3):
                for copy in early[kind, group]:
                    copy.wait_recv()
            lax.fori_loop(first, last, moment_plane, 0)

        for at in range(3):
            for copy in late_copies[at * (nodes - 1) : (at + 1) * (nodes - 1)]:
                copy.wait_recv()
            late_moment_plane(at, 0)

    early_copies = late_copies + [copy for copies in early.values() for copy in copies]
    for copy in [x_down, x_up, near_down, near_up, far_down, far_up, q_down, q_up]:
        copy.wait_send()
    for copy in [*scalar_copies, *note_copies, *early_copies]:
        copy.wait_send()


def per_device(nodes, slabs, probes, potential, warm_start, shift_points, quad_weights):
    depth, width, length = potential.shape
    block = width // nodes
    narrow = block % 16 == 0
    f32, bf16 = jnp.float32, jnp.bfloat16
    anywhere = pl.BlockSpec(memory_space=pltpu.HBM)
    scalars = pl.BlockSpec(memory_space=pltpu.SMEM)
    vector = pl.BlockSpec(memory_space=pltpu.VMEM)
    dma = pltpu.SemaphoreType.DMA
    return pl.pallas_call(
        functools.partial(kernel, nodes, slabs),
        out_shape=(
            jax.ShapeDtypeStruct((2, 1, 2, depth, block, length), f32),
            jax.ShapeDtypeStruct((2,), f32),
        ),
        in_specs=[anywhere] * 7,
        out_specs=(vector, scalars),
        scratch_shapes=[
            pltpu.VMEM((2, depth + 4, width, length), bf16),
            pltpu.VMEM((depth, width, length), f32),
            pltpu.VMEM((depth, width, length), f32),
            pltpu.VMEM((2, depth + 4, width, length), f32),
            pltpu.VMEM((2, depth + 2, width, length), f32),
            pltpu.VMEM((2, width, length), f32),
            pltpu.VMEM((SUMS, 8, length), f32),
            pltpu.VMEM((slabs, SUMS, 128), f32),
            pltpu.VMEM((2, 2, width, length), bf16),
            pltpu.VMEM((2, 2, width, length), bf16),
            pltpu.VMEM((2, 2, 2, width // 2, length), bf16),
            pltpu.VMEM((2, 2, 2, width // 2, length), bf16),
            pltpu.VMEM((8, 128) if narrow else (2, depth, width, length), f32),
            pltpu.VMEM((nodes, 2, depth, block, length), bf16 if narrow else f32),
            pltpu.VMEM((nodes, 2, depth, block, length), f32),
            pltpu.VMEM((nodes, 2, depth, block, length), f32),
            pltpu.VMEM((3, 2, width, length), f32),
            pltpu.VMEM((nodes, 3, 2, block, length), f32),
            pltpu.VMEM((nodes, 16, 128), f32),
            pltpu.SMEM((1, 2), f32),
            pltpu.SMEM((1, 2), f32),
            pltpu.VMEM((width, width), bf16),
            pltpu.VMEM((length, length), bf16),
            dma((7,)),
            dma((2,)),
            dma((2,)),
            dma((2,)),
            dma((2,)),
            dma((2,)),
            dma((2,)),
            dma((slabs,)),
            dma((slabs,)),
            dma((nodes,)),
            dma((nodes,)),
            dma((2,)),
            dma((2,)),
            dma((nodes, 9)),
            dma((nodes, 9)),
        ],
        compiler_params=pltpu.CompilerParams(
            collective_id=0, has_side_effects=True, vmem_limit_bytes=64 * 1024 * 1024
        ),
    )(
        warm_start,
        probes,
        potential,
        shift_points,
        quad_weights,
        jnp.asarray(ring_matrix(width, 0.0)),
        jnp.asarray(ring_matrix(length, -90.0)),
    )


def solution(mesh):
    return jax.shard_map(
        functools.partial(per_device, mesh.shape["node"], mesh.shape["grid"]),
        mesh=mesh,
        in_specs=(
            P(None, "grid", None, None),
            P("grid", None, None),
            P("node", None, None, "grid", None, None),
            P("node", None),
            P("node", None),
        ),
        out_specs=(P(None, None, None, "grid", "node", None), P()),
        check_vma=False,
    )
```

profile of v0, /device:TPU:0, one launch (start us, length us, event | category | flops | bytes accessed | tf_op | source)
XLA Modules:
  0.0 64.0 jit_solution(9525886012665301437)
XLA Ops:
  0.6 60.4 %shard_map.86 = (f32[2,1,2,6,48,256]{5,4,3,2,1,0:T(8,128)}, f32[2]{0:T(128)}) custom-call(bf16[1,1,2,6,192,256]{5,4,3,2,1,0:T(8,128)(2,1)} %warm.1, f32[1,6,192,256]{3,2,1,0:T(8,128)} %probes.1, f32[6,192,256]{2,1,0:T(8,128)} %potential.1, f32[1,2]{1,0:T(1,128)} %shift_hbm.1, f32[1,2]{1,0:T(1,128)} %weight_hbm.1, ...), custom_call_target="tpu_custom_call" | custom-call | tf_op jit(solution)/shard_map/pallas_call | solution.py:538
  61.0 0.0 copy-start
  61.1 2.4 %copy.11 = f32[2,1,2,6,48,256]{5,4,3,2,1,0:T(8,128)} copy(f32[2,1,2,6,48,256]{5,4,3,2,1,0:T(8,128)} %get-tuple-element.4) | data formatting | bytes 2359296
  63.4 0.0 copy-done
  63.4 0.5 copy.12
Async XLA Ops:
  61.0 2.4 %copy-start = (f32[2]{0:T(128)S(1)}, f32[2]{0:T(128)}, u32[]{:S(2)}) copy-start(f32[2]{0:T(128)} %get-tuple-element.5) | copy-start | bytes 28
where the time goes:
time: 64.1 us; the launch traced here: 64 us
  Pallas kernels  60.4 us (94%)
  local copies, waits for them, and re-layouts  2.9 us (5%)
  between operations  0.65 us (1%)
    pallas_call x1, Pallas kernels, per_device(): pl.pallas_call(functools.partial(kernel, nodes, slabs), out_shape=(jax.Sh...  60.4 us
    unnamed x4, local copies, waits for them, and re-layouts  2.9 us

commit v1 on v0

v1 whole, which is shorter than its diff:
```python
import functools

import jax
import jax.numpy as jnp
import ml_dtypes
import numpy as np
from jax import lax
from jax.experimental import pallas as pl
from jax.experimental.pallas import tpu as pltpu
from jax.sharding import PartitionSpec as P

MESH = pl.DeviceIdType.MESH
SUMS = 16
NEAR, FAR = 16.0, -1.0


def up_to(size, step):
    return -(-size // step) * step


def weight_of(distance):
    return {1: NEAR, 2: FAR}.get(abs(distance), 0.0)


def ring_matrix(size, diagonal):
    matrix = np.zeros((size, size), np.float32)
    at = np.arange(size)
    for step, weight in ((1, NEAR), (2, FAR)):
        matrix[at, (at + step) % size] += weight
        matrix[at, (at - step) % size] += weight
    matrix[at, at] += diagonal
    return matrix.astype(ml_dtypes.bfloat16)


def table(block):
    tall = up_to(block, 16)
    sizes = {
        "own": (tall, tall),
        "halo0": (tall, 16),
        "halo1": (tall, 16),
        "split0": (tall, 2 * block + 16),
        "split1": (tall, 2 * block + 16),
        "ahead": (tall, 2 * block),
        "edge_own": (16, 2 * tall),
        "edge_halo": (16, 48),
        "cross": (16, 16),
    }
    at, places = 0, {}
    for name, (rows, cols) in sizes.items():
        places[name] = (at, rows, cols)
        at += rows
    return places, at, up_to(max(cols for rows, cols in sizes.values()), 128)


def small_matrices(block, depth):
    tall = up_to(block, 16)
    places, rows, cols = table(block)
    whole = np.zeros((rows, cols), np.float32)
    view = {name: whole[at : at + n, :m] for name, (at, n, m) in places.items()}
    wide = [-4, -3, -2, -1, block, block + 1, block + 2, block + 3]
    slim = [-2, -1, block, block + 1]
    for i in range(block):
        for j in range(block):
            w = weight_of(i - j)
            view["own"][i, j] = w
            for s in range(2):
                view[f"split{s}"][i, j] = w
                view[f"split{s}"][i, block + j] = w
            if j > i:
                view["ahead"][i, j] = 2 * w
                view["ahead"][i, block + j] = 2 * w
        for s in range(2):
            for c, x in enumerate(wide):
                view[f"halo{s}"][i, 8 * s + c] = weight_of(i - x)
            for c, x in enumerate(slim):
                view[f"split{s}"][i, 2 * block + 4 * s + c] = weight_of(i - x)
                view[f"split{s}"][i, 2 * block + 8 + 4 * s + c] = weight_of(i - x)
    for s in range(2):
        for t, x in enumerate(slim):
            row, here = 4 * s + t, wide.index(x)
            for j in range(block):
                view["edge_own"][row, tall * s + j] = weight_of(x - j)
            for c, other in enumerate(wide):
                view["edge_halo"][row, 16 + 8 * s + c] += weight_of(x - other)
            for q in range(6):
                view["edge_halo"][row, 8 * q + here] += weight_of(q - 2 - s)
            view["edge_halo"][8 + row, 16 + 8 * s + here] = 1.0
    for p in range(depth):
        for e in range(2):
            for f in range(2):
                view["cross"][2 * p + e, 2 * p + f] = 2 * weight_of(2 - e + f)
    return whole.astype(ml_dtypes.bfloat16)


def halo_picks(width, nodes):
    block = width // nodes
    picks = np.zeros((nodes * 16, 2 * width), np.float32)
    for m in range(nodes):
        for s in range(2):
            for c, x in enumerate([-4, -3, -2, -1, block, block + 1, block + 2, block + 3]):
                picks[16 * m + 8 * s + c, width * s + (block * m + x) % width] = 1.0
    return picks.astype(ml_dtypes.bfloat16)


def core_picks(width, nodes):
    block = width // nodes
    tall = up_to(block, 16)
    picks = np.zeros((nodes * tall, width), np.float32)
    for m in range(nodes):
        for i in range(block):
            picks[tall * m + i, block * m + i] = 1.0
    return picks.astype(ml_dtypes.bfloat16)


def cmul(a, b):
    return a[0] * b[0] - a[1] * b[1], a[0] * b[1] + a[1] * b[0]


def cdiv(a, b):
    size = b[0] * b[0] + b[1] * b[1]
    return (a[0] * b[0] + a[1] * b[1]) / size, (a[1] * b[0] - a[0] * b[1]) / size


def fold(values):
    rows, cols = values.shape
    return jnp.sum(values.reshape(rows // 8, 8, cols), axis=0)


def dot(a, b):
    return jnp.dot(a, b, preferred_element_type=jnp.float32)


def kernel(
    nodes,
    slabs,
    warm,
    probes,
    potential,
    shift_hbm,
    weight_hbm,
    along_y_hbm,
    small_hbm,
    picks_hbm,
    core_hbm,
    moments,
    trace,
    own,
    hsend,
    csend,
    wbuf,
    halo,
    bbuf,
    vbuf,
    bside,
    vside,
    bedge,
    vedge,
    rbuf,
    redge,
    qbuf,
    qfirst,
    qlast,
    qhead,
    qahead,
    edge_out,
    edge_in,
    acc,
    sums,
    totals,
    notes,
    shift_ref,
    weight_ref,
    along_y,
    small,
    picks,
    cpicks,
    local_sem,
    b_send,
    b_recv,
    a_send,
    a_recv,
    z_send,
    z_recv,
    q_send,
    q_recv,
    x_send,
    x_recv,
    s_send,
    s_recv,
    t_send,
    t_recv,
):
    f32, bf16 = jnp.float32, jnp.bfloat16
    node, slab = lax.axis_index("node"), lax.axis_index("grid")
    depth, width, length = own.shape[1:]
    pairs = depth // 2
    block = width // nodes
    tall = up_to(block, 16)
    narrow = block % 16 == 0
    lower = nodes // 2
    places = table(block)[0]
    above = (node, lax.rem(slab + 1, slabs))
    below = (node, lax.rem(slab + slabs - 1, slabs))
    step = 16 if narrow else 8
    mine = pl.ds(pl.multiple_of(node * block, step), block)
    left = pl.ds(pl.multiple_of(lax.rem(node * block + width - 8, width), 8), 8)
    right = pl.ds(pl.multiple_of(lax.rem(node * block + block, width), 8), 8)

    def matrix(name):
        at, rows, cols = places[name]
        return small[at : at + rows, 0:cols]

    loads = []

    def load(source, target):
        copy = pltpu.make_async_copy(source, target, local_sem.at[len(loads)])
        copy.start()
        loads.append(copy)

    load(shift_hbm, shift_ref)
    load(weight_hbm, weight_ref)
    load(warm.at[0, 0], own)
    load(picks_hbm, picks)
    if not narrow:
        load(core_hbm, cpicks)
    first_loads = len(loads)
    load(along_y_hbm, along_y)
    load(small_hbm, small)
    load(probes.at[0, :, mine], bbuf.at[2 : depth + 2])
    load(potential.at[:, mine], vbuf.at[2 : depth + 2])
    load(probes.at[0, :, left], bside.at[0])
    load(probes.at[0, :, right], bside.at[1])
    load(potential.at[:, left], vside.at[0])
    load(potential.at[:, right], vside.at[1])
    if narrow:
        load(warm.at[0, 0, :, :, mine], wbuf.at[0, :, 4 : depth + 4])

    barrier = pltpu.get_barrier_semaphore()
    for k in range(1, slabs):
        pl.semaphore_signal(
            barrier, inc=1, device_id=(node, lax.rem(slab + k, slabs)), device_id_type=MESH
        )
    for k in range(1, nodes):
        pl.semaphore_signal(
            barrier, inc=1, device_id=(lax.rem(node + k, nodes), slab), device_id_type=MESH
        )
    pl.semaphore_wait(barrier, slabs + nodes - 2)

    def remote(source, target, send_sem, recv_sem, device):
        return pltpu.make_async_remote_copy(
            src_ref=source,
            dst_ref=target,
            send_sem=send_sem,
            recv_sem=recv_sem,
            device_id=device,
            device_id_type=MESH,
        )

    def peer(k):
        return lax.rem(node + k, nodes)

    def core(m, first, last):
        if narrow:
            rows = pl.ds(pl.multiple_of(m * block, step), block)
            return warm.at[0, 0, :, first:last, rows]
        return csend.at[m, :, first:last]

    chunks = ((0, 2), (depth - 2, depth), (2, depth - 2))

    def gather_copy(k, c):
        first, last = chunks[c]
        return remote(
            core(peer(k), first, last),
            wbuf.at[k, :, 4 + first : 4 + last],
            a_send.at[k, c],
            a_recv.at[k, c],
            (peer(k), slab),
        )

    def halo_copy(k):
        return remote(
            hsend.at[peer(k)],
            halo.at[k, :, 1 : pairs + 1],
            a_send.at[k, 3],
            a_recv.at[k, 3],
            (peer(k), slab),
        )

    def note_copy(k):
        return remote(notes.at[0], notes.at[k], a_send.at[k, 4], a_recv.at[k, 4], (peer(k), slab))

    top = depth + 4
    routes = (
        ((4, 6), (top, top + 2), below),
        ((top - 2, top), (2, 4), above),
        ((6, 8), (top + 2, top + 4), below),
        ((top - 4, top - 2), (0, 2), above),
    )

    def forward(k, c):
        source, target, device = routes[c]
        if isinstance(k, int) and k == 0:
            part = core(node, source[0] - 4, source[1] - 4)
        else:
            part = wbuf.at[k, :, source[0] : source[1]]
        return remote(
            part, wbuf.at[k, :, target[0] : target[1]], z_send.at[k, c], z_recv.at[k, c], device
        )

    def forward_halo(k, c):
        source, target, device = ((1, pairs + 1, below), (pairs, 0, above))[c]
        return remote(
            halo.at[k, :, source],
            halo.at[k, :, target],
            z_send.at[k, 4 + c],
            z_recv.at[k, 4 + c],
            device,
        )

    sides = []
    for at, (source, target) in enumerate(((probes.at[0], bbuf), (potential, vbuf))):
        for c, (first, there, device) in enumerate(
            ((0, depth + 2, below), (depth - 2, 0, above))
        ):
            sides.append(
                remote(
                    source.at[first : first + 2, mine],
                    target.at[there : there + 2],
                    b_send.at[2 * at + c],
                    b_recv.at[2 * at + c],
                    device,
                )
            )

    def pick():
        for copy in loads[2:first_loads]:
            copy.wait()
        for i in range(pairs):
            for part in range(2):
                rows = own[part, 2 * i : 2 * i + 2].reshape(2 * width, length)
                picked = dot(picks[...], rows).astype(bf16)
                for m in range(nodes):
                    hsend[m, part, i] = picked[16 * m : 16 * m + 16]
        if not narrow:
            for part in range(2):
                for p in range(depth):
                    picked = dot(cpicks[...], own[part, p]).astype(bf16)
                    for m in range(nodes):
                        csend[m, part, p] = picked[tall * m : tall * m + tall]

    def send_cores():
        for c in range(3):
            for k in range(1, nodes):
                gather_copy(k, c).start()
        for c in range(4):
            forward(0, c).start()
            if c == 1:
                for copy in sides:
                    copy.start()

    if narrow:
        send_cores()
    for copy in loads[0:2]:
        copy.wait()
    row = lax.broadcasted_iota(jnp.int32, (8, length), 0)
    note = jnp.zeros((8, length), f32)
    entries = (shift_ref[0, 0], shift_ref[0, 1], weight_ref[0, 0], weight_ref[0, 1])
    for i, entry in enumerate(entries):
        note = jnp.where(row == i, entry, note)
    notes[0] = note
    for k in range(1, nodes):
        note_copy(k).start()
    pick()
    if not narrow:
        send_cores()
    for k in range(1, nodes):
        halo_copy(k).start()
    for part in range(2):
        for i in range(pairs):
            halo[0, part, 1 + i] = hsend[node, part, i]
    for c in range(2):
        forward_halo(0, c).start()
    if not narrow:
        for part in range(2):
            for p in range(depth):
                wbuf[0, part, 4 + p] = csend[node, part, p]

    acc[...] = jnp.zeros_like(acc)
    qfirst[...] = jnp.zeros_like(qfirst)
    qlast[...] = jnp.zeros_like(qlast)
    qbuf[lower:nodes, :, depth : depth + 2] = jnp.zeros((nodes - lower, 2, 2, block, length), f32)
    for copy in loads[first_loads:]:
        copy.wait()
    for i in range(pairs):
        for s in range(2):
            for side in range(2):
                there = 4 * s + 2 * side
                here = 6 if side == 0 else 0
                bedge[i, there : there + 2] = bside[side, 2 * i + s, here : here + 2]
                vedge[i, there : there + 2] = vside[side, 2 * i + s, here : here + 2]

    def shift_of(k):
        return notes[k, 0:1, :], notes[k, 1:2, :]

    def apply(shift, field, stencil, local):
        diagonal = shift[0] - local
        return (
            diagonal * field[0] - shift[1] * field[1] + stencil[0] * (1.0 / 24.0),
            diagonal * field[1] + shift[1] * field[0] + stencil[1] * (1.0 / 24.0),
        )

    def added(k, first, count, low, high, terms):
        def body(i, carry):
            for s in range(2):
                carry = tuple(c + fold(v) for c, v in zip(carry, terms(i, s)))
            return carry

        zero = jnp.zeros((8, length), f32)
        for i, total in enumerate(lax.fori_loop(low, high, body, (zero,) * count)):
            acc[k * SUMS + first + i] += total

    def wide(values):
        return values.astype(f32)[0:block]

    def residual(k, i, s):
        pp = 2 * i + s
        stencil, field = [], []
        for part in range(2):
            centre = wbuf[k, part, pp + 2]
            plane = (
                dot(centre, along_y[...])
                + dot(matrix("own"), centre)
                + dot(matrix(f"halo{s}"), halo[k, part, i])
            )[0:block]
            at = [wide(wbuf[k, part, pp + j]) for j in (0, 1, 3, 4)]
            stencil.append(plane + 16.0 * (at[1] + at[2]) - (at[0] + at[3]))
            field.append(wide(centre))
        source = bbuf[pp]
        image = apply(shift_of(k), field, stencil, vbuf[pp])
        r = source - image[0], -image[1]
        rbuf[k, 0, pp] = r[0]
        rbuf[k, 1, pp] = r[1]
        return source, field, r

    def residual_terms(k, i, s):
        source, field, r = residual(k, i, s)
        return (
            r[0] * r[0] - r[1] * r[1],
            2.0 * r[0] * r[1],
            source * field[0],
            source * field[1],
            source * r[0],
            source * r[1],
        )

    def edge_pair(k, i):
        stencil, field = [], []
        for part in range(2):
            middle = wbuf[k, part, pl.ds(4 + 2 * i, 2)].reshape(2 * tall, length)
            around = halo[k, part, pl.ds(i, 3)].reshape(48, length)
            both = dot(matrix("edge_halo"), around)
            plane = dot(both.astype(bf16), along_y[...])
            beside = dot(matrix("edge_own"), middle)
            stencil.append(beside[0:8] + both[0:8] + plane[8:16])
            field.append(both[8:16])
        image = apply(shift_of(k), field, stencil, vedge[i])
        redge[k, 0, i] = bedge[i] - image[0]
        redge[k, 1, i] = -image[1]

    def split(values):
        high = values.astype(bf16)
        return high, (values - high.astype(f32)).astype(bf16)

    def pack(values):
        high, low = split(values)
        if narrow:
            return jnp.concatenate([high, low], axis=0)
        return jnp.concatenate([high.astype(f32), low.astype(f32)], axis=0).astype(bf16)

    def slim(values):
        high, low = split(values)
        return jnp.concatenate([high.astype(f32), low.astype(f32)], axis=0).astype(bf16)

    def along(packed):
        both = dot(packed, along_y[...])
        return both[0:block] + both[block : 2 * block]

    def image_terms(k, i, s):
        p = 2 * i + s
        stencil, field = [], []
        for part in range(2):
            at = [rbuf[k, part, p + j] for j in range(5)]
            packed = pack(at[2])
            side = jnp.concatenate([packed, slim(redge[k, part, i])], axis=0)
            plane = along(packed) + dot(matrix(f"split{s}"), side)[0:block]
            stencil.append(plane + 16.0 * (at[1] + at[3]) - (at[0] + at[4]))
            field.append(at[2])
        source = bbuf[p + 2]
        q = apply(shift_of(k), field, stencil, vbuf[p + 2])
        qbuf[k, 0, p] = q[0]
        qbuf[k, 1, p] = q[1]
        return (
            *cmul(field, q),
            q[0] * q[0] - q[1] * q[1],
            2.0 * q[0] * q[1],
            source * q[0],
            source * q[1],
        )

    def energy_terms(k, i, s):
        p = 2 * i + s
        stencil, field = [], []
        for part in range(2):
            at = [qbuf[k, part, p + j] for j in range(3)]
            packed = pack(at[0])
            plane = along(packed) + dot(matrix("ahead"), packed)[0:block]
            stencil.append(plane + 32.0 * at[1] - 2.0 * at[2])
            field.append(at[0])
        return cmul(field, apply(shift_of(k), field, stencil, vbuf[p + 2]))

    def own_step(k, carry):
        @pl.when(k == 1)
        def _():
            for c in range(2):
                for j in range(1, nodes):
                    gather_copy(j, c).wait_recv()
                    forward(j, c).start()
            for j in range(1, nodes):
                note_copy(j).wait_recv()
                halo_copy(j).wait_recv()
                for c in range(2):
                    forward_halo(j, c).start()
            for j in range(1, nodes):
                gather_copy(j, 2).wait_recv()
                for c in range(2, 4):
                    forward(j, c).start()

        for c in range(2):
            forward(k, c).wait_recv()
            forward_halo(k, c).wait_recv()
        added(k, 0, 6, 1, pairs + 1, functools.partial(residual_terms, k))

        def edges(i, inner):
            edge_pair(k, i)
            return inner

        lax.fori_loop(0, pairs, edges, 0)
        added(k, 6, 6, 1, pairs - 1, functools.partial(image_terms, k))
        return carry

    with jax.named_scope("residual"):
        lax.fori_loop(0, nodes, own_step, 0)

    for copy in sides:
        copy.wait_recv()

    def q_copy(k, down):
        if down:
            return remote(
                edge_out.at[k], edge_in.at[k], q_send.at[k], q_recv.at[k], below
            )
        return remote(edge_out.at[k], edge_in.at[k], q_send.at[k], q_recv.at[k], above)

    def x_copy(k):
        there = lax.rem(k + nodes - 1, nodes)
        return remote(
            qhead.at[k], qahead.at[there], x_send.at[k], x_recv.at[there], (peer(nodes - 1), slab)
        )

    def x_arrival(k):
        return remote(
            qhead.at[k], qahead.at[k], x_send.at[k], x_recv.at[k], (peer(nodes - 1), slab)
        )

    def outer_step(k, carry):
        for c in range(2, 4):
            forward(k, c).wait_recv()

        def outer(j, inner):
            for s in range(2):
                residual(k, j * (pairs + 1), s)
            return inner

        lax.fori_loop(0, 2, outer, 0)

        def ends(j, s):
            return image_terms(k, j * (pairs - 1), s)

        added(k, 6, 6, 0, 2, ends)

        def narrowed(first):
            for part in range(2):
                for p in range(2):
                    values = qbuf[k, part, first + p]
                    if narrow:
                        edge_out[k, part, p] = values.astype(bf16)
                    else:
                        filler = jnp.zeros((tall - block, length), f32)
                        edge_out[k, part, p] = jnp.concatenate([values, filler], axis=0).astype(bf16)

        @pl.when(k < lower)
        def _():
            narrowed(0)
            q_copy(k, True).start()

        @pl.when(k >= lower)
        def _():
            narrowed(depth - 2)
            q_copy(k, False).start()

        for part in range(2):
            for p in range(depth):
                qfirst[k, part, 2 * p : 2 * p + 2] = qbuf[k, part, p, 0:2]
                qlast[k, part, 2 * p : 2 * p + 2] = qbuf[k, part, p, block - 2 : block]
            qhead[k, part] = qfirst[k, part].astype(bf16)
        x_copy(k).start()
        return carry

    with jax.named_scope("image"):
        lax.fori_loop(0, nodes, outer_step, 0)

    def energy_step(k, carry):
        @pl.when(k < lower)
        def _():
            q_copy(k, True).wait_recv()
            for part in range(2):
                for p in range(2):
                    qbuf[k, part, depth + p] = wide(edge_in[k, part, p])

        added(k, 12, 2, 0, pairs, functools.partial(energy_terms, k))
        x_arrival(k).wait_recv()
        last = [qlast[k, part] for part in range(2)]
        ahead = [dot(matrix("cross"), qahead[k, part]) for part in range(2)]
        crossing = cmul(last, ahead)
        for part in range(2):
            acc[k * SUMS + 12 + part] += fold(crossing[part] * (1.0 / 24.0))

        @pl.when(k >= lower)
        def _():
            q_copy(k, False).wait_recv()
            near = [wide(edge_in[k, part, 1]) for part in range(2)]
            far = [wide(edge_in[k, part, 0]) for part in range(2)]
            zeroth = [qbuf[k, part, 0] for part in range(2)]
            first = [qbuf[k, part, 1] for part in range(2)]
            one = cmul(zeroth, [32.0 * near[part] - 2.0 * far[part] for part in range(2)])
            two = cmul(first, near)
            for part in range(2):
                acc[k * SUMS + 12 + part] += fold((one[part] - 2.0 * two[part]) * (1.0 / 24.0))

        return carry

    with jax.named_scope("energy"):
        lax.fori_loop(0, nodes, energy_step, 0)

    with jax.named_scope("scalars"):
        lane = lax.broadcasted_iota(jnp.int32, (SUMS, 128), 1)
        shift_at = [lax.rem(node - k + nodes, nodes) for k in range(nodes)]
        mine_sum = jnp.zeros((SUMS, 128), f32)
        for k in range(nodes):
            partial = jnp.sum(acc[k * SUMS : (k + 1) * SUMS], axis=1)
            lanes = partial[:, 0:128]
            for at in range(128, length, 128):
                lanes = lanes + partial[:, at : at + 128]
            whole = jnp.sum(lanes, axis=1, keepdims=True)
            mine_sum = mine_sum + jnp.where(lane == shift_at[k], whole, 0.0)
        sums[0] = mine_sum
        slab_copies = [
            remote(
                sums.at[0],
                sums.at[k],
                s_send.at[k],
                s_recv.at[k],
                (node, lax.rem(slab + k, slabs)),
            )
            for k in range(1, slabs)
        ]
        for copy in slab_copies:
            copy.start()
        for copy in slab_copies:
            copy.wait_recv()
        total = jnp.zeros((SUMS, 128), f32)
        for owner in range(slabs):
            total = total + sums[lax.rem(slab - owner + slabs, slabs)]
        totals[0] = total
        node_copies = [
            remote(totals.at[0], totals.at[k], t_send.at[k], t_recv.at[k], (peer(k), slab))
            for k in range(1, nodes)
        ]
        for copy in node_copies:
            copy.start()
        for copy in node_copies:
            copy.wait_recv()
        total = jnp.zeros((SUMS, 128), f32)
        for owner in range(nodes):
            total = total + totals[lax.rem(node - owner + nodes, nodes)]
        pair = lambda i: (total[i : i + 1], total[i + 1 : i + 2])
        s0, t0, t1, s1, s2, t2, s3 = (pair(i) for i in range(0, 14, 2))
        row_lane = lax.broadcasted_iota(jnp.int32, (8, 128), 1)
        known = jnp.zeros((8, 128), f32)
        for k in range(nodes):
            known = known + jnp.where(row_lane == shift_at[k], notes[k][:, 0:128], 0.0)
        shift = known[0:1], known[1:2]
        weight = known[2:3], known[3:4]
        step0 = cdiv(s0, s1)
        square = cmul(step0, step0)
        norm1 = cmul(square, s2)
        norm1 = norm1[0] - s0[0], norm1[1] - s0[1]
        ratio = cdiv(norm1, s0)
        grow = ratio[0] + 1.0, ratio[1]
        one = cmul(cmul(grow, grow), s1)
        two = cmul(cmul(grow, step0), s2)
        three = cmul(square, s3)
        step1 = cdiv(
            norm1, (one[0] - 2.0 * two[0] + three[0], one[1] - 2.0 * two[1] + three[1])
        )
        coef_r = cmul(step1, grow)
        coef_r = coef_r[0] + step0[0], coef_r[1] + step0[1]
        coef_q = cmul(step1, step0)
        coef_q = -coef_q[0], -coef_q[1]
        inner_r, inner_q = cmul(coef_r, t1), cmul(coef_q, t2)
        inner = t0[0] + inner_r[0] + inner_q[0], t0[1] + inner_r[1] + inner_q[1]
        share = cmul(weight, inner)
        following = cmul(weight, ((shift[0] - 4.0) * 0.2, shift[1] * 0.2))
        sub = lax.broadcasted_iota(jnp.int32, (SUMS, 128), 0)
        factors = jnp.zeros((SUMS, 128), f32)
        for i, entry in enumerate((*weight, *following, *share, *coef_r, *coef_q)):
            factors = jnp.where(sub == i, entry, factors)
        for part in range(2):
            trace[part] = jnp.sum(jnp.where((sub == 4 + part) & (lane < nodes), factors, 0.0))

    with jax.named_scope("moments"):
        scale = []
        for k in range(nodes):
            one_lane = jnp.where(lane == shift_at[k], factors, 0.0)
            values = jnp.broadcast_to(jnp.sum(one_lane, axis=1, keepdims=True), (SUMS, length))
            scale.append([(values[i : i + 1], values[i + 1 : i + 2]) for i in (0, 2, 6, 8)])
        piece = 16 if narrow else block

        def moment_plane(p, carry):
            def step(i, inner_carry):
                rows = pl.ds(pl.multiple_of(i * piece, piece), piece)
                values = [None] * 4
                for k in range(nodes):
                    if narrow:
                        x = [wbuf[k, part, p + 4, rows].astype(f32) for part in range(2)]
                    else:
                        x = [wide(wbuf[k, part, p + 4]) for part in range(2)]
                    r = [rbuf[k, part, p + 2, rows] for part in range(2)]
                    q = [qbuf[k, part, p, rows] for part in range(2)]
                    along_r, along_q = cmul(scale[k][2], r), cmul(scale[k][3], q)
                    field = [x[part] + along_r[part] + along_q[part] for part in range(2)]
                    for degree in range(2):
                        term = cmul(scale[k][degree], field)
                        for part in range(2):
                            at = 2 * degree + part
                            values[at] = term[part] if k == 0 else values[at] + term[part]
                for degree in range(2):
                    for part in range(2):
                        moments[degree, 0, part, p, rows] = values[2 * degree + part]
                return inner_carry

            lax.fori_loop(0, block // piece, step, 0)
            return carry

        lax.fori_loop(0, depth, moment_plane, 0)

    for copy in [*sides, *slab_copies, *node_copies]:
        copy.wait_send()
    for k in range(nodes):
        if k:
            for c in range(3):
                gather_copy(k, c).wait_send()
            halo_copy(k).wait_send()
            note_copy(k).wait_send()
        for c in range(4):
            forward(k, c).wait_send()
        for c in range(2):
            forward_halo(k, c).wait_send()
        q_copy(k, k < lower).wait_send()
        x_copy(k).wait_send()


def per_device(nodes, slabs, probes, potential, warm_start, shift_points, quad_weights):
    depth, width, length = potential.shape
    block = width // nodes
    tall = up_to(block, 16)
    narrow = block % 16 == 0
    pairs = depth // 2
    f32, bf16 = jnp.float32, jnp.bfloat16
    anywhere = pl.BlockSpec(memory_space=pltpu.HBM)
    vector = pl.BlockSpec(memory_space=pltpu.VMEM)
    scalars = pl.BlockSpec(memory_space=pltpu.SMEM)
    dma = pltpu.SemaphoreType.DMA
    small = small_matrices(block, depth)
    picks = halo_picks(width, nodes)
    cpicks = np.zeros((16, 128), ml_dtypes.bfloat16) if narrow else core_picks(width, nodes)
    return pl.pallas_call(
        functools.partial(kernel, nodes, slabs),
        out_shape=(
            jax.ShapeDtypeStruct((2, 1, 2, depth, block, length), f32),
            jax.ShapeDtypeStruct((2,), f32),
        ),
        in_specs=[anywhere] * 9,
        out_specs=(vector, scalars),
        scratch_shapes=[
            pltpu.VMEM((2, depth, width, length), bf16),
            pltpu.VMEM((nodes, 2, pairs, 16, length), bf16),
            pltpu.VMEM((16, 128) if narrow else (nodes, 2, depth, tall, length), bf16),
            pltpu.VMEM((nodes, 2, depth + 8, tall, length), bf16),
            pltpu.VMEM((nodes, 2, pairs + 2, 16, length), bf16),
            pltpu.VMEM((depth + 4, block, length), f32),
            pltpu.VMEM((depth + 4, block, length), f32),
            pltpu.VMEM((2, depth, 8, length), f32),
            pltpu.VMEM((2, depth, 8, length), f32),
            pltpu.VMEM((pairs, 8, length), f32),
            pltpu.VMEM((pairs, 8, length), f32),
            pltpu.VMEM((nodes, 2, depth + 4, block, length), f32),
            pltpu.VMEM((nodes, 2, pairs, 8, length), f32),
            pltpu.VMEM((nodes, 2, depth + 2, block, length), f32),
            pltpu.VMEM((nodes, 2, 16, length), f32),
            pltpu.VMEM((nodes, 2, 16, length), f32),
            pltpu.VMEM((nodes, 2, 16, length), bf16),
            pltpu.VMEM((nodes, 2, 16, length), bf16),
            pltpu.VMEM((nodes, 2, 2, tall, length), bf16),
            pltpu.VMEM((nodes, 2, 2, tall, length), bf16),
            pltpu.VMEM((nodes * SUMS, 8, length), f32),
            pltpu.VMEM((slabs, SUMS, 128), f32),
            pltpu.VMEM((nodes, SUMS, 128), f32),
            pltpu.VMEM((nodes, 8, length), f32),
            pltpu.SMEM((1, 2), f32),
            pltpu.SMEM((1, 2), f32),
            pltpu.VMEM((length, length), bf16),
            pltpu.VMEM(small.shape, bf16),
            pltpu.VMEM(picks.shape, bf16),
            pltpu.VMEM(cpicks.shape, bf16),
            dma((14,)),
            dma((4,)),
            dma((4,)),
            dma((nodes, 5)),
            dma((nodes, 5)),
            dma((nodes, 6)),
            dma((nodes, 6)),
            dma((nodes,)),
            dma((nodes,)),
            dma((nodes,)),
            dma((nodes,)),
            dma((slabs,)),
            dma((slabs,)),
            dma((nodes,)),
            dma((nodes,)),
        ],
        compiler_params=pltpu.CompilerParams(
            collective_id=0, has_side_effects=True, vmem_limit_bytes=60 * 1024 * 1024
        ),
    )(
        warm_start,
        probes,
        potential,
        shift_points,
        quad_weights,
        jnp.asarray(ring_matrix(length, -90.0)),
        jnp.asarray(small),
        jnp.asarray(picks),
        jnp.asarray(cpicks),
    )


def solution(mesh):
    return jax.shard_map(
        functools.partial(per_device, mesh.shape["node"], mesh.shape["grid"]),
        mesh=mesh,
        in_specs=(
            P(None, "grid", None, None),
            P("grid", None, None),
            P("node", None, None, "grid", None, None),
            P("node", None),
            P("node", None),
        ),
        out_specs=(P(None, None, None, "grid", "node", None), P()),
        check_vma=False,
    )
```

time: 64.1 us -> 58 us (0.905)
  Pallas kernels: 60.4 us -> 53.7 us
    pallas_call x1, Pallas kernels: 60.4 us -> 53.7 us  [per_device(): pl.pallas_call(functools.partial(kernel, nodes, slabs), out_shape=(jax.Sh...]
where the time goes in v1:
time: 58 us; the launch traced here: 57.9 us
  Pallas kernels  53.7 us (93%)
  local copies, waits for them, and re-layouts  3.49 us (6%)
  between operations  0.65 us (1%)
    pallas_call x1, Pallas kernels, per_device(): pl.pallas_call(functools.partial(kernel, nodes, slabs), out_shape=(jax.Sh...  53.7 us
    unnamed x4, local copies, waits for them, and re-layouts  2.9 us

profile of v1, /device:TPU:0, one launch (start us, length us, event | category | flops | bytes accessed | tf_op | source)
XLA Modules:
  0.0 57.9 jit_solution(9415967412128262136)
XLA Ops:
  0.6 0.6 %jit_solution_.3.core_hbm = bf16[16,128]{1,0:T(8,128)(2,1)} broadcast(bf16[]{:T(256)} %constant.11.clone), dimensions={} | broadcast | bytes 4098 | tf_op jit(solution)
  1.2 53.7 %shard_map.104 = (f32[2,1,2,6,48,256]{5,4,3,2,1,0:T(8,128)}, f32[2]{0:T(128)}) custom-call(bf16[1,1,2,6,192,256]{5,4,3,2,1,0:T(8,128)(2,1)} %warm.1, f32[1,6,192,256]{3,2,1,0:T(8,128)} %probes.1, f32[6,192,256]{2,1,0:T(8,128)} %potential.1, f32[1,2]{1,0:T(1,128)} %shift_hbm.1, f32[1,2]{1,0:T(1,128)} %weight_hbm.1, ...), custom_call_target="tpu_custom_call" | custom-call | tf_op jit(solution)/shard_map/pallas_call | solution.py:797
  55.0 0.0 copy-start
  55.0 2.4 %copy.13 = f32[2,1,2,6,48,256]{5,4,3,2,1,0:T(8,128)} copy(f32[2,1,2,6,48,256]{5,4,3,2,1,0:T(8,128)} %get-tuple-element.4) | data formatting | bytes 2359296
  57.3 0.0 copy-done
  57.3 0.5 copy.14
Async XLA Ops:
  55.0 2.4 %copy-start = (f32[2]{0:T(128)S(1)}, f32[2]{0:T(128)}, u32[]{:S(2)}) copy-start(f32[2]{0:T(128)} %get-tuple-element.5) | copy-start | bytes 28

commit v2 on v1

--- a/solution.py
+++ b/solution.py
@@ -32,8 +32,9 @@
     return matrix.astype(ml_dtypes.bfloat16)
 
 
-def table(block):
+def table(block, depth):
     tall = up_to(block, 16)
+    pairs = depth // 2
     sizes = {
         "own": (tall, tall),
         "halo0": (tall, 16),
@@ -42,7 +43,7 @@
         "split1": (tall, 2 * block + 16),
         "ahead": (tall, 2 * block),
         "edge_own": (16, 2 * tall),
-        "edge_halo": (16, 48),
+        "edge_halo": (16 * pairs, 16 * (pairs + 2)),
         "cross": (16, 16),
     }
     at, places = 0, {}
@@ -54,7 +55,7 @@
 
 def small_matrices(block, depth):
     tall = up_to(block, 16)
-    places, rows, cols = table(block)
+    places, rows, cols = table(block, depth)
     whole = np.zeros((rows, cols), np.float32)
     view = {name: whole[at : at + n, :m] for name, (at, n, m) in places.items()}
     wide = [-4, -3, -2, -1, block, block + 1, block + 2, block + 3]
@@ -80,11 +81,13 @@
             row, here = 4 * s + t, wide.index(x)
             for j in range(block):
                 view["edge_own"][row, tall * s + j] = weight_of(x - j)
-            for c, other in enumerate(wide):
-                view["edge_halo"][row, 16 + 8 * s + c] += weight_of(x - other)
-            for q in range(6):
-                view["edge_halo"][row, 8 * q + here] += weight_of(q - 2 - s)
-            view["edge_halo"][8 + row, 16 + 8 * s + here] = 1.0
+            for i in range(depth // 2):
+                to, at = 8 * i + row, 16 * i
+                for c, other in enumerate(wide):
+                    view["edge_halo"][to, at + 16 + 8 * s + c] += weight_of(x - other)
+                for q in range(6):
+                    view["edge_halo"][to, at + 8 * q + here] += weight_of(q - 2 - s)
+                view["edge_halo"][4 * depth + to, at + 16 + 8 * s + here] = 1.0
     for p in range(depth):
         for e in range(2):
             for f in range(2):
@@ -157,6 +160,8 @@
     vedge,
     rbuf,
     redge,
+    far_out,
+    far_in,
     qbuf,
     qfirst,
     qlast,
@@ -198,7 +203,7 @@
     tall = up_to(block, 16)
     narrow = block % 16 == 0
     lower = nodes // 2
-    places = table(block)[0]
+    places = table(block, depth)[0]
     above = (node, lax.rem(slab + 1, slabs))
     below = (node, lax.rem(slab + slabs - 1, slabs))
     step = 16 if narrow else 8
@@ -293,8 +298,8 @@
     routes = (
         ((4, 6), (top, top + 2), below),
         ((top - 2, top), (2, 4), above),
-        ((6, 8), (top + 2, top + 4), below),
-        ((top - 4, top - 2), (0, 2), above),
+        ((6, 7), (top + 2, top + 3), below),
+        ((top - 3, top - 2), (1, 2), above),
     )
 
     def forward(k, c):
@@ -320,17 +325,22 @@
     sides = []
     for at, (source, target) in enumerate(((probes.at[0], bbuf), (potential, vbuf))):
         for c, (first, there, device) in enumerate(
-            ((0, depth + 2, below), (depth - 2, 0, above))
+            ((0, depth + 2, below), (depth - 1, 1, above))
         ):
             sides.append(
                 remote(
-                    source.at[first : first + 2, mine],
-                    target.at[there : there + 2],
+                    source.at[first : first + 1, mine],
+                    target.at[there : there + 1],
                     b_send.at[2 * at + c],
                     b_recv.at[2 * at + c],
                     device,
                 )
             )
+
+    def far_copy(k, c):
+        return remote(
+            far_out.at[k, c], far_in.at[k, c], z_send.at[k, 6 + c], z_recv.at[k, 6 + c], routes[c][2]
+        )
 
     def pick():
         for copy in loads[2:first_loads]:
@@ -394,10 +404,10 @@
     for i in range(pairs):
         for s in range(2):
             for side in range(2):
-                there = 4 * s + 2 * side
+                there = 8 * i + 4 * s + 2 * side
                 here = 6 if side == 0 else 0
-                bedge[i, there : there + 2] = bside[side, 2 * i + s, here : here + 2]
-                vedge[i, there : there + 2] = vside[side, 2 * i + s, here : here + 2]
+                bedge[there : there + 2] = bside[side, 2 * i + s, here : here + 2]
+                vedge[there : there + 2] = vside[side, 2 * i + s, here : here + 2]
 
     def shift_of(k):
         return notes[k, 0:1, :], notes[k, 1:2, :]
@@ -453,19 +463,22 @@
             source * r[1],
         )
 
-    def edge_pair(k, i):
+    def edge_rows(k):
         stencil, field = [], []
         for part in range(2):
-            middle = wbuf[k, part, pl.ds(4 + 2 * i, 2)].reshape(2 * tall, length)
-            around = halo[k, part, pl.ds(i, 3)].reshape(48, length)
+            around = halo[k, part].reshape(16 * (pairs + 2), length)
             both = dot(matrix("edge_halo"), around)
             plane = dot(both.astype(bf16), along_y[...])
-            beside = dot(matrix("edge_own"), middle)
-            stencil.append(beside[0:8] + both[0:8] + plane[8:16])
-            field.append(both[8:16])
-        image = apply(shift_of(k), field, stencil, vedge[i])
-        redge[k, 0, i] = bedge[i] - image[0]
-        redge[k, 1, i] = -image[1]
+            beside = [
+                dot(matrix("edge_own"), wbuf[k, part, 4 + 2 * i : 6 + 2 * i].reshape(2 * tall, length))
+                for i in range(pairs)
+            ]
+            beside = jnp.concatenate([rows[0:8] for rows in beside], axis=0)
+            stencil.append(beside + both[0 : 4 * depth] + plane[4 * depth :])
+            field.append(both[4 * depth :])
+        image = apply(shift_of(k), field, stencil, vedge[...])
+        redge[k, 0] = bedge[...] - image[0]
+        redge[k, 1] = -image[1]
 
     def split(values):
         high = values.astype(bf16)
@@ -491,7 +504,7 @@
         for part in range(2):
             at = [rbuf[k, part, p + j] for j in range(5)]
             packed = pack(at[2])
-            side = jnp.concatenate([packed, slim(redge[k, part, i])], axis=0)
+            side = jnp.concatenate([packed, slim(redge[k, part, pl.ds(pl.multiple_of(8 * i, 8), 8)])], axis=0)
             plane = along(packed) + dot(matrix(f"split{s}"), side)[0:block]
             stencil.append(plane + 16.0 * (at[1] + at[3]) - (at[0] + at[4]))
             field.append(at[2])
@@ -517,6 +530,12 @@
             stencil.append(plane + 32.0 * at[1] - 2.0 * at[2])
             field.append(at[0])
         return cmul(field, apply(shift_of(k), field, stencil, vbuf[p + 2]))
+
+    def narrowed(values):
+        if not narrow:
+            filler = jnp.zeros((tall - block, length), f32)
+            values = jnp.concatenate([values, filler], axis=0)
+        return values.astype(bf16)
 
     def own_step(k, carry):
         @pl.when(k == 1)
@@ -540,11 +559,11 @@
             forward_halo(k, c).wait_recv()
         added(k, 0, 6, 1, pairs + 1, functools.partial(residual_terms, k))
 
-        def edges(i, inner):
-            edge_pair(k, i)
-            return inner
-
-        lax.fori_loop(0, pairs, edges, 0)
+        for c, at in enumerate((3, depth)):
+            for part in range(2):
+                far_out[k, c, part] = narrowed(rbuf[k, part, at])
+            far_copy(k, c).start()
+        edge_rows(k)
         added(k, 6, 6, 1, pairs - 1, functools.partial(image_terms, k))
         return carry
 
@@ -576,36 +595,31 @@
         for c in range(2, 4):
             forward(k, c).wait_recv()
 
-        def outer(j, inner):
-            for s in range(2):
-                residual(k, j * (pairs + 1), s)
-            return inner
-
-        lax.fori_loop(0, 2, outer, 0)
+        residual(k, 0, 1)
+        residual(k, pairs + 1, 0)
+        for c, at in enumerate((depth + 3, 0)):
+            far_copy(k, c).wait_recv()
+            for part in range(2):
+                rbuf[k, part, at] = wide(far_in[k, c, part])
 
         def ends(j, s):
             return image_terms(k, j * (pairs - 1), s)
 
         added(k, 6, 6, 0, 2, ends)
 
-        def narrowed(first):
+        def share_q(first):
             for part in range(2):
                 for p in range(2):
-                    values = qbuf[k, part, first + p]
-                    if narrow:
-                        edge_out[k, part, p] = values.astype(bf16)
-                    else:
-                        filler = jnp.zeros((tall - block, length), f32)
-                        edge_out[k, part, p] = jnp.concatenate([values, filler], axis=0).astype(bf16)
+                    edge_out[k, part, p] = narrowed(qbuf[k, part, first + p])
 
         @pl.when(k < lower)
         def _():
-            narrowed(0)
+            share_q(0)
             q_copy(k, True).start()
 
         @pl.when(k >= lower)
         def _():
-            narrowed(depth - 2)
+            share_q(depth - 2)
             q_copy(k, False).start()
 
         for part in range(2):
@@ -776,6 +790,7 @@
             forward(k, c).wait_send()
         for c in range(2):
             forward_halo(k, c).wait_send()
+            far_copy(k, c).wait_send()
         q_copy(k, k < lower).wait_send()
         x_copy(k).wait_send()
 
@@ -793,11 +808,11 @@
     dma = pltpu.SemaphoreType.DMA
     small = small_matrices(block, depth)
     picks = halo_picks(width, nodes)
-    cpicks = np.zeros((16, 128), ml_dtypes.bfloat16) if narrow else core_picks(width, nodes)
+    cpicks = picks if narrow else core_picks(width, nodes)
     return pl.pallas_call(
         functools.partial(kernel, nodes, slabs),
         out_shape=(
-            jax.ShapeDtypeStruct((2, 1, 2, depth, block, length), f32),
+            pltpu.VMEM((2, 1, 2, depth, block, length), f32),
             jax.ShapeDtypeStruct((2,), f32),
         ),
         in_specs=[anywhere] * 9,
@@ -812,10 +827,12 @@
             pltpu.VMEM((depth + 4, block, length), f32),
             pltpu.VMEM((2, depth, 8, length), f32),
             pltpu.VMEM((2, depth, 8, length), f32),
-            pltpu.VMEM((pairs, 8, length), f32),
-            pltpu.VMEM((pairs, 8, length), f32),
+            pltpu.VMEM((4 * depth, length), f32),
+            pltpu.VMEM((4 * depth, length), f32),
             pltpu.VMEM((nodes, 2, depth + 4, block, length), f32),
-            pltpu.VMEM((nodes, 2, pairs, 8, length), f32),
+            pltpu.VMEM((nodes, 2, 4 * depth, length), f32),
+            pltpu.VMEM((nodes, 2, 2, tall, length), bf16),
+            pltpu.VMEM((nodes, 2, 2, tall, length), bf16),
             pltpu.VMEM((nodes, 2, depth + 2, block, length), f32),
             pltpu.VMEM((nodes, 2, 16, length), f32),
             pltpu.VMEM((nodes, 2, 16, length), f32),
@@ -832,14 +849,14 @@
             pltpu.VMEM((length, length), bf16),
             pltpu.VMEM(small.shape, bf16),
             pltpu.VMEM(picks.shape, bf16),
-            pltpu.VMEM(cpicks.shape, bf16),
+            pltpu.VMEM((16, 128) if narrow else cpicks.shape, bf16),
             dma((14,)),
             dma((4,)),
             dma((4,)),
             dma((nodes, 5)),
             dma((nodes, 5)),
-            dma((nodes, 6)),
-            dma((nodes, 6)),
+            dma((nodes, 8)),
+            dma((nodes, 8)),
             dma((nodes,)),
             dma((nodes,)),
             dma((nodes,)),
@@ -850,7 +867,7 @@
             dma((nodes,)),
         ],
         compiler_params=pltpu.CompilerParams(
-            collective_id=0, has_side_effects=True, vmem_limit_bytes=60 * 1024 * 1024
+            collective_id=0, has_side_effects=True, vmem_limit_bytes=58 * 1024 * 1024
         ),
     )(
         warm_start,

time: 58 us -> 51.5 us (0.89)
  Pallas kernels: 53.7 us -> 49.2 us
  local copies, waits for them, and re-layouts: 3.49 us -> 1.53 us
    pallas_call x1, Pallas kernels: 53.7 us -> 49.2 us  [per_device(): pl.pallas_call(functools.partial(kernel, nodes, slabs), out_shape=(pltpu....]
    unnamed x4, local copies, waits for them, and re-layouts: 2.9 us -> 1.53 us
    another operation x1 -> x0, local copies, waits for them, and re-layouts: 0.6 us -> none
where the time goes in v2:
time: 51.5 us; the launch traced here: 51.3 us
  Pallas kernels  49.2 us (96%)
  local copies, waits for them, and re-layouts  1.53 us (3%)
  between operations  0.65 us (1%)
    pallas_call x1, Pallas kernels, per_device(): pl.pallas_call(functools.partial(kernel, nodes, slabs), out_shape=(pltpu....  49.2 us
    unnamed x4, local copies, waits for them, and re-layouts  1.53 us

profile of v2, /device:TPU:0, one launch (start us, length us, event | category | flops | bytes accessed | tf_op | source)
XLA Modules:
  0.0 51.3 jit_solution(17329424758963473619)
XLA Ops:
  0.6 49.2 %shard_map.95 = (f32[2,1,2,6,48,256]{5,4,3,2,1,0:T(8,128)S(1)}, f32[2]{0:T(128)}) custom-call(bf16[1,1,2,6,192,256]{5,4,3,2,1,0:T(8,128)(2,1)} %warm.1, f32[1,6,192,256]{3,2,1,0:T(8,128)} %probes.1, f32[6,192,256]{2,1,0:T(8,128)} %potential.1, f32[1,2]{1,0:T(1,128)} %shift_hbm.1, f32[1,2]{1,0:T(1,128)} %weight_hbm.1, ...), custom_call_target="tpu_custom_call" | custom-call | tf_op jit(solution)/shard_map/pallas_call | solution.py:812
  49.8 0.0 copy-start
  49.8 1.0 %copy.12 = f32[2,1,2,6,48,256]{5,4,3,2,1,0:T(8,128)} copy(f32[2,1,2,6,48,256]{5,4,3,2,1,0:T(8,128)S(1)} %get-tuple-element.2) | data formatting | bytes 2359296
  50.8 0.0 copy-done
  50.8 0.5 copy.13
Async XLA Ops:
  49.8 1.0 %copy-start = (f32[2]{0:T(128)S(1)}, f32[2]{0:T(128)}, u32[]{:S(2)}) copy-start(f32[2]{0:T(128)} %get-tuple-element.7) | copy-start | bytes 28

commit v3 on v2

--- a/solution.py
+++ b/solution.py
@@ -115,6 +115,11 @@
     return picks.astype(ml_dtypes.bfloat16)
 
 
+def offsets(nodes):
+    every = [(a, b) for a in range(nodes // 2) for b in range(2)]
+    return [(0, 0)] + sorted(every[1:], key=lambda at: -(at[0] > 0) - (at[1] > 0))
+
+
 def cmul(a, b):
     return a[0] * b[0] - a[1] * b[1], a[0] * b[1] + a[1] * b[0]
 
@@ -171,7 +176,6 @@
     edge_in,
     acc,
     sums,
-    totals,
     notes,
     shift_ref,
     weight_ref,
@@ -192,8 +196,6 @@
     x_recv,
     s_send,
     s_recv,
-    t_send,
-    t_recv,
 ):
     f32, bf16 = jnp.float32, jnp.bfloat16
     node, slab = lax.axis_index("node"), lax.axis_index("grid")
@@ -261,8 +263,18 @@
             device_id_type=MESH,
         )
 
+    steps = offsets(nodes)
+    distant = sum(1 for a, b in steps if a and b)
+    tall_y = nodes // 2
+    at_y, at_x = node // 2, lax.rem(node, 2)
+
     def peer(k):
-        return lax.rem(node + k, nodes)
+        a, b = steps[k]
+        return lax.rem(at_y + a, tall_y) * 2 + lax.rem(at_x + b, 2)
+
+    def owner_of(k):
+        a, b = steps[k]
+        return lax.rem(at_y + tall_y - a, tall_y) * 2 + lax.rem(at_x + b, 2)
 
     def core(m, first, last):
         if narrow:
@@ -341,6 +353,8 @@
         return remote(
             far_out.at[k, c], far_in.at[k, c], z_send.at[k, 6 + c], z_recv.at[k, 6 + c], routes[c][2]
         )
+
+    order = [(k, c) for c in range(3) for k in range(1, nodes)]
 
     def pick():
         for copy in loads[2:first_loads]:
@@ -359,14 +373,12 @@
                         csend[m, part, p] = picked[tall * m : tall * m + tall]
 
     def send_cores():
-        for c in range(3):
-            for k in range(1, nodes):
-                gather_copy(k, c).start()
+        for k, c in order:
+            gather_copy(k, c).start()
         for c in range(4):
             forward(0, c).start()
-            if c == 1:
-                for copy in sides:
-                    copy.start()
+        for copy in sides:
+            copy.start()
 
     if narrow:
         send_cores()
@@ -540,19 +552,16 @@
     def own_step(k, carry):
         @pl.when(k == 1)
         def _():
-            for c in range(2):
-                for j in range(1, nodes):
-                    gather_copy(j, c).wait_recv()
-                    forward(j, c).start()
-            for j in range(1, nodes):
-                note_copy(j).wait_recv()
-                halo_copy(j).wait_recv()
-                for c in range(2):
-                    forward_halo(j, c).start()
-            for j in range(1, nodes):
-                gather_copy(j, 2).wait_recv()
-                for c in range(2, 4):
-                    forward(j, c).start()
+            for at, (j, c) in enumerate(order):
+                if at == 2 * (nodes - 1):
+                    for m in range(1, nodes):
+                        note_copy(m).wait_recv()
+                        halo_copy(m).wait_recv()
+                        for d in range(2):
+                            forward_halo(m, d).start()
+                gather_copy(j, c).wait_recv()
+                for d in (c,) if c < 2 else (2, 3):
+                    forward(j, d).start()
 
         for c in range(2):
             forward(k, c).wait_recv()
@@ -573,6 +582,8 @@
     for copy in sides:
         copy.wait_recv()
 
+    previous = lax.rem(node + nodes - 1, nodes)
+
     def q_copy(k, down):
         if down:
             return remote(
@@ -581,14 +592,16 @@
         return remote(edge_out.at[k], edge_in.at[k], q_send.at[k], q_recv.at[k], above)
 
     def x_copy(k):
-        there = lax.rem(k + nodes - 1, nodes)
+        a, b = steps[k]
+        same, before = steps.index((a, 1 - b)), steps.index(((a - 1) % tall_y, 1 - b))
+        there = at_x * same + (1 - at_x) * before
         return remote(
-            qhead.at[k], qahead.at[there], x_send.at[k], x_recv.at[there], (peer(nodes - 1), slab)
+            qhead.at[k], qahead.at[there], x_send.at[k], x_recv.at[there], (previous, slab)
         )
 
     def x_arrival(k):
         return remote(
-            qhead.at[k], qahead.at[k], x_send.at[k], x_recv.at[k], (peer(nodes - 1), slab)
+            qhead.at[k], qahead.at[k], x_send.at[k], x_recv.at[k], (previous, slab)
         )
 
     def outer_step(k, carry):
@@ -627,11 +640,12 @@
                 qfirst[k, part, 2 * p : 2 * p + 2] = qbuf[k, part, p, 0:2]
                 qlast[k, part, 2 * p : 2 * p + 2] = qbuf[k, part, p, block - 2 : block]
             qhead[k, part] = qfirst[k, part].astype(bf16)
-        x_copy(k).start()
         return carry
 
     with jax.named_scope("image"):
         lax.fori_loop(0, nodes, outer_step, 0)
+        for k in range(nodes):
+            x_copy(k).start()
 
     def energy_step(k, carry):
         @pl.when(k < lower)
@@ -642,13 +656,6 @@
                     qbuf[k, part, depth + p] = wide(edge_in[k, part, p])
 
         added(k, 12, 2, 0, pairs, functools.partial(energy_terms, k))
-        x_arrival(k).wait_recv()
-        last = [qlast[k, part] for part in range(2)]
-        ahead = [dot(matrix("cross"), qahead[k, part]) for part in range(2)]
-        crossing = cmul(last, ahead)
-        for part in range(2):
-            acc[k * SUMS + 12 + part] += fold(crossing[part] * (1.0 / 24.0))
-
         @pl.when(k >= lower)
         def _():
             q_copy(k, False).wait_recv()
@@ -663,50 +670,94 @@
 
         return carry
 
+    def cross_step(k, carry):
+        x_arrival(k).wait_recv()
+        last = [qlast[k, part] for part in range(2)]
+        ahead = [dot(matrix("cross"), qahead[k, part]) for part in range(2)]
+        crossing = cmul(last, ahead)
+        for part in range(2):
+            acc[k * SUMS + 12 + part] += fold(crossing[part] * (1.0 / 24.0))
+        return carry
+
     with jax.named_scope("energy"):
         lax.fori_loop(0, nodes, energy_step, 0)
+        lax.fori_loop(0, nodes, cross_step, 0)
+
+    piece = 16 if narrow else block
+    factor = []
+    for k in range(nodes):
+        shift, weight = shift_of(k), (notes[k, 2:3, :], notes[k, 3:4, :])
+        scaled = (shift[0] - 4.0) * 0.2, shift[1] * 0.2
+        factor.append((weight, scaled, cmul(weight, scaled)))
+
+    def rows_of(p, step):
+        def body(i, carry):
+            rows = pl.ds(pl.multiple_of(i * piece, piece), piece)
+            values = step(p, rows)
+            for degree in range(2):
+                for part in range(2):
+                    moments[degree, 0, part, p, rows] = values[2 * degree + part]
+            return carry
+
+        lax.fori_loop(0, block // piece, body, 0)
+
+    def start_rows(p, rows):
+        values = [None] * 4
+        for k in range(nodes):
+            if narrow:
+                x = [wbuf[k, part, p + 4, rows].astype(f32) for part in range(2)]
+            else:
+                x = [wide(wbuf[k, part, p + 4]) for part in range(2)]
+            for degree in range(2):
+                term = cmul(factor[k][2 * degree], x)
+                for part in range(2):
+                    at = 2 * degree + part
+                    values[at] = term[part] if k == 0 else values[at] + term[part]
+        return values
+
+    def start_plane(p, carry):
+        rows_of(p, start_rows)
+        return carry
 
     with jax.named_scope("scalars"):
         lane = lax.broadcasted_iota(jnp.int32, (SUMS, 128), 1)
-        shift_at = [lax.rem(node - k + nodes, nodes) for k in range(nodes)]
-        mine_sum = jnp.zeros((SUMS, 128), f32)
+        shift_at = [owner_of(k) for k in range(nodes)]
+        sub = lax.broadcasted_iota(jnp.int32, (SUMS, 128), 0)
+        per_row = 128 // SUMS
+        spread = [jnp.zeros((SUMS, 128), f32) for _ in range(sums.shape[1])]
         for k in range(nodes):
             partial = jnp.sum(acc[k * SUMS : (k + 1) * SUMS], axis=1)
             lanes = partial[:, 0:128]
             for at in range(128, length, 128):
                 lanes = lanes + partial[:, at : at + 128]
             whole = jnp.sum(lanes, axis=1, keepdims=True)
-            mine_sum = mine_sum + jnp.where(lane == shift_at[k], whole, 0.0)
-        sums[0] = mine_sum
-        slab_copies = [
-            remote(
-                sums.at[0],
-                sums.at[k],
-                s_send.at[k],
-                s_recv.at[k],
-                (node, lax.rem(slab + k, slabs)),
-            )
-            for k in range(1, slabs)
-        ]
-        for copy in slab_copies:
+            for row in range(len(spread)):
+                there = (shift_at[k] - row * per_row) * SUMS + sub
+                spread[row] = spread[row] + jnp.where(lane == there, whole, 0.0)
+        me = node * slabs + slab
+        for row, values in enumerate(spread):
+            sums[me, row : row + 1] = jnp.sum(values, axis=0, keepdims=True)
+        scalar_copies = []
+        for a in range(nodes):
+            for b in range(slabs):
+                if a or b:
+                    there = lax.rem(node + a, nodes), lax.rem(slab + b, slabs)
+                    at = a * slabs + b
+                    scalar_copies.append(
+                        remote(sums.at[me], sums.at[me], s_send.at[at], s_recv.at[at], there)
+                    )
+        for copy in scalar_copies:
             copy.start()
-        for copy in slab_copies:
+        lax.fori_loop(0, depth, start_plane, 0)
+        for copy in scalar_copies:
             copy.wait_recv()
-        total = jnp.zeros((SUMS, 128), f32)
-        for owner in range(slabs):
-            total = total + sums[lax.rem(slab - owner + slabs, slabs)]
-        totals[0] = total
-        node_copies = [
-            remote(totals.at[0], totals.at[k], t_send.at[k], t_recv.at[k], (peer(k), slab))
-            for k in range(1, nodes)
-        ]
-        for copy in node_copies:
-            copy.start()
-        for copy in node_copies:
-            copy.wait_recv()
+        every = jnp.sum(sums[...], axis=0)
         total = jnp.zeros((SUMS, 128), f32)
         for owner in range(nodes):
-            total = total + totals[lax.rem(node - owner + nodes, nodes)]
+            row = owner // per_row
+            wide_row = jnp.broadcast_to(every[row : row + 1], (SUMS, 128))
+            picked = jnp.where(lane == (owner - row * per_row) * SUMS + sub, wide_row, 0.0)
+            total = total + jnp.where(lane == owner, jnp.sum(picked, axis=1, keepdims=True), 0.0)
         pair = lambda i: (total[i : i + 1], total[i + 1 : i + 2])
         s0, t0, t1, s1, s2, t2, s3 = (pair(i) for i in range(0, 14, 2))
         row_lane = lax.broadcasted_iota(jnp.int32, (8, 128), 1)
@@ -735,7 +786,6 @@
         inner = t0[0] + inner_r[0] + inner_q[0], t0[1] + inner_r[1] + inner_q[1]
         share = cmul(weight, inner)
         following = cmul(weight, ((shift[0] - 4.0) * 0.2, shift[1] * 0.2))
-        sub = lax.broadcasted_iota(jnp.int32, (SUMS, 128), 0)
         factors = jnp.zeros((SUMS, 128), f32)
         for i, entry in enumerate((*weight, *following, *share, *coef_r, *coef_q)):
             factors = jnp.where(sub == i, entry, factors)
@@ -747,38 +797,29 @@
         for k in range(nodes):
             one_lane = jnp.where(lane == shift_at[k], factors, 0.0)
             values = jnp.broadcast_to(jnp.sum(one_lane, axis=1, keepdims=True), (SUMS, length))
-            scale.append([(values[i : i + 1], values[i + 1 : i + 2]) for i in (0, 2, 6, 8)])
-        piece = 16 if narrow else block
+            along_r, along_q = ((values[i : i + 1], values[i + 1 : i + 2]) for i in (6, 8))
+            scale.append((cmul(factor[k][0], along_r), cmul(factor[k][0], along_q)))
+
+        def moment_rows(p, rows):
+            values = [moments[degree, 0, part, p, rows] for degree in range(2) for part in range(2)]
+            for k in range(nodes):
+                r = [rbuf[k, part, p + 2, rows] for part in range(2)]
+                q = [qbuf[k, part, p, rows] for part in range(2)]
+                along_r, along_q = cmul(scale[k][0], r), cmul(scale[k][1], q)
+                field = [along_r[part] + along_q[part] for part in range(2)]
+                term = cmul(factor[k][1], field)
+                for part in range(2):
+                    values[part] = values[part] + field[part]
+                    values[2 + part] = values[2 + part] + term[part]
+            return values
 
         def moment_plane(p, carry):
-            def step(i, inner_carry):
-                rows = pl.ds(pl.multiple_of(i * piece, piece), piece)
-                values = [None] * 4
-                for k in range(nodes):
-                    if narrow:
-                        x = [wbuf[k, part, p + 4, rows].astype(f32) for part in range(2)]
-                    else:
-                        x = [wide(wbuf[k, part, p + 4]) for part in range(2)]
-                    r = [rbuf[k, part, p + 2, rows] for part in range(2)]
-                    q = [qbuf[k, part, p, rows] for part in range(2)]
-                    along_r, along_q = cmul(scale[k][2], r), cmul(scale[k][3], q)
-                    field = [x[part] + along_r[part] + along_q[part] for part in range(2)]
-                    for degree in range(2):
-                        term = cmul(scale[k][degree], field)
-                        for part in range(2):
-                            at = 2 * degree + part
-                            values[at] = term[part] if k == 0 else values[at] + term[part]
-                for degree in range(2):
-                    for part in range(2):
-                        moments[degree, 0, part, p, rows] = values[2 * degree + part]
-                return inner_carry
-
-            lax.fori_loop(0, block // piece, step, 0)
+            rows_of(p, moment_rows)
             return carry
 
         lax.fori_loop(0, depth, moment_plane, 0)
 
-    for copy in [*sides, *slab_copies, *node_copies]:
+    for copy in [*sides, *scalar_copies]:
         copy.wait_send()
     for k in range(nodes):
         if k:
@@ -841,8 +882,7 @@
             pltpu.VMEM((nodes, 2, 2, tall, length), bf16),
             pltpu.VMEM((nodes, 2, 2, tall, length), bf16),
             pltpu.VMEM((nodes * SUMS, 8, length), f32),
-            pltpu.VMEM((slabs, SUMS, 128), f32),
-            pltpu.VMEM((nodes, SUMS, 128), f32),
+            pltpu.VMEM((nodes * slabs, up_to(nodes * SUMS, 128) // 128, 128), f32),
             pltpu.VMEM((nodes, 8, length), f32),
             pltpu.SMEM((1, 2), f32),
             pltpu.SMEM((1, 2), f32),
@@ -861,10 +901,8 @@
             dma((nodes,)),
             dma((nodes,)),
             dma((nodes,)),
-            dma((slabs,)),
-            dma((slabs,)),
-            dma((nodes,)),
-            dma((nodes,)),
+            dma((nodes * slabs,)),
+            dma((nodes * slabs,)),
         ],
         compiler_params=pltpu.CompilerParams(
             collective_id=0, has_side_effects=True, vmem_limit_bytes=58 * 1024 * 1024

time: 51.5 us -> 49.4 us (0.959)
  Pallas kernels: 49.2 us -> 47.1 us
    pallas_call x1, Pallas kernels: 49.2 us -> 47.1 us  [per_device(): pl.pallas_call(functools.partial(kernel, nodes, slabs), out_shape=(pltpu....]
where the time goes in v3:
time: 49.4 us; the launch traced here: 49.3 us
  Pallas kernels  47.1 us (95%)
  local copies, waits for them, and re-layouts  1.53 us (3%)
  between operations  0.65 us (1%)
    pallas_call x1, Pallas kernels, per_device(): pl.pallas_call(functools.partial(kernel, nodes, slabs), out_shape=(pltpu....  47.1 us
    unnamed x4, local copies, waits for them, and re-layouts  1.53 us

profile of v3, /device:TPU:0, one launch (start us, length us, event | category | flops | bytes accessed | tf_op | source)
XLA Modules:
  0.0 49.3 jit_solution(17271676339785978472)
XLA Ops:
  0.6 47.1 %shard_map.95 = (f32[2,1,2,6,48,256]{5,4,3,2,1,0:T(8,128)S(1)}, f32[2]{0:T(128)}) custom-call(bf16[1,1,2,6,192,256]{5,4,3,2,1,0:T(8,128)(2,1)} %warm.1, f32[1,6,192,256]{3,2,1,0:T(8,128)} %probes.1, f32[6,192,256]{2,1,0:T(8,128)} %potential.1, f32[1,2]{1,0:T(1,128)} %shift_hbm.1, f32[1,2]{1,0:T(1,128)} %weight_hbm.1, ...), custom_call_target="tpu_custom_call" | custom-call | tf_op jit(solution)/shard_map/pallas_call | solution.py:853
  47.7 0.0 copy-start
  47.7 1.0 %copy.12 = f32[2,1,2,6,48,256]{5,4,3,2,1,0:T(8,128)} copy(f32[2,1,2,6,48,256]{5,4,3,2,1,0:T(8,128)S(1)} %get-tuple-element.2) | data formatting | bytes 2359296
  48.7 0.0 copy-done
  48.7 0.5 %copy.13 = f32[2]{0:T(128)} copy(f32[2]{0:T(128)S(1)} %copy-done) | data formatting | bytes 16
Async XLA Ops:
  47.7 1.0 %copy-start = (f32[2]{0:T(128)S(1)}, f32[2]{0:T(128)}, u32[]{:S(2)}) copy-start(f32[2]{0:T(128)} %get-tuple-element.7) | copy-start | bytes 28

commit v4 on v3

--- a/solution.py
+++ b/solution.py
@@ -151,7 +151,10 @@
     picks_hbm,
     core_hbm,
     moments,
-    trace,
+    rbuf,
+    qbuf,
+    scale_out,
+    table_out,
     own,
     hsend,
     csend,
@@ -163,11 +166,9 @@
     vside,
     bedge,
     vedge,
-    rbuf,
     redge,
     far_out,
     far_in,
-    qbuf,
     qfirst,
     qlast,
     qhead,
@@ -374,7 +375,8 @@
 
     def send_cores():
         for k, c in order:
-            gather_copy(k, c).start()
+            if c < 2 or not narrow:
+                gather_copy(k, c).start()
         for c in range(4):
             forward(0, c).start()
         for copy in sides:
@@ -397,6 +399,10 @@
         send_cores()
     for k in range(1, nodes):
         halo_copy(k).start()
+    if narrow:
+        for k, c in order:
+            if c == 2:
+                gather_copy(k, c).start()
     for part in range(2):
         for i in range(pairs):
             halo[0, part, 1 + i] = hsend[node, part, i]
@@ -572,12 +578,16 @@
             for part in range(2):
                 far_out[k, c, part] = narrowed(rbuf[k, part, at])
             far_copy(k, c).start()
+        return carry
+
+    def inner_step(k, carry):
         edge_rows(k)
         added(k, 6, 6, 1, pairs - 1, functools.partial(image_terms, k))
         return carry
 
     with jax.named_scope("residual"):
         lax.fori_loop(0, nodes, own_step, 0)
+        lax.fori_loop(0, nodes, inner_step, 0)
 
     for copy in sides:
         copy.wait_recv()
@@ -640,12 +650,14 @@
                 qfirst[k, part, 2 * p : 2 * p + 2] = qbuf[k, part, p, 0:2]
                 qlast[k, part, 2 * p : 2 * p + 2] = qbuf[k, part, p, block - 2 : block]
             qhead[k, part] = qfirst[k, part].astype(bf16)
+        for j in range(nodes):
+            @pl.when(k == j)
+            def _():
+                x_copy(j).start()
         return carry
 
     with jax.named_scope("image"):
         lax.fori_loop(0, nodes, outer_step, 0)
-        for k in range(nodes):
-            x_copy(k).start()
 
     def energy_step(k, carry):
         @pl.when(k < lower)
@@ -789,35 +801,14 @@
         factors = jnp.zeros((SUMS, 128), f32)
         for i, entry in enumerate((*weight, *following, *share, *coef_r, *coef_q)):
             factors = jnp.where(sub == i, entry, factors)
-        for part in range(2):
-            trace[part] = jnp.sum(jnp.where((sub == 4 + part) & (lane < nodes), factors, 0.0))
-
-    with jax.named_scope("moments"):
-        scale = []
+        table_out[...] = factors
         for k in range(nodes):
             one_lane = jnp.where(lane == shift_at[k], factors, 0.0)
             values = jnp.broadcast_to(jnp.sum(one_lane, axis=1, keepdims=True), (SUMS, length))
             along_r, along_q = ((values[i : i + 1], values[i + 1 : i + 2]) for i in (6, 8))
-            scale.append((cmul(factor[k][0], along_r), cmul(factor[k][0], along_q)))
-
-        def moment_rows(p, rows):
-            values = [moments[degree, 0, part, p, rows] for degree in range(2) for part in range(2)]
-            for k in range(nodes):
-                r = [rbuf[k, part, p + 2, rows] for part in range(2)]
-                q = [qbuf[k, part, p, rows] for part in range(2)]
-                along_r, along_q = cmul(scale[k][0], r), cmul(scale[k][1], q)
-                field = [along_r[part] + along_q[part] for part in range(2)]
-                term = cmul(factor[k][1], field)
-                for part in range(2):
-                    values[part] = values[part] + field[part]
-                    values[2 + part] = values[2 + part] + term[part]
-            return values
-
-        def moment_plane(p, carry):
-            rows_of(p, moment_rows)
-            return carry
-
-        lax.fori_loop(0, depth, moment_plane, 0)
+            entries = (*factor[k][1], *cmul(factor[k][0], along_r), *cmul(factor[k][0], along_q))
+            for i, entry in enumerate(entries):
+                scale_out[k, i : i + 1] = entry
 
     for copy in [*sides, *scalar_copies]:
         copy.wait_send()
@@ -836,6 +827,52 @@
         x_copy(k).wait_send()
 
 
+def finish(nodes, started, rbuf, qbuf, scales, factors, moments, trace, result, pair, sems):
+    depth, block, length = result.shape[2:]
+    piece = 16 if block % 16 == 0 else block
+    scale = []
+    for k in range(nodes):
+        rows = [scales[k, i : i + 1, :] for i in range(6)]
+        scale.append((rows[0:2], rows[2:4], rows[4:6]))
+
+    def copy(p):
+        return pltpu.make_async_copy(result.at[:, :, p], moments.at[:, 0, :, p], sems.at[p])
+
+    def plane(p, carry):
+        def body(i, inner):
+            rows = pl.ds(pl.multiple_of(i * piece, piece), piece)
+            values = [started[degree, 0, part, p, rows] for degree in range(2) for part in range(2)]
+            for k in range(nodes):
+                r = [rbuf[k, part, p + 2, rows] for part in range(2)]
+                q = [qbuf[k, part, p, rows] for part in range(2)]
+                along_r, along_q = cmul(scale[k][1], r), cmul(scale[k][2], q)
+                field = [along_r[part] + along_q[part] for part in range(2)]
+                term = cmul(scale[k][0], field)
+                for part in range(2):
+                    values[part] = values[part] + field[part]
+                    values[2 + part] = values[2 + part] + term[part]
+            for degree in range(2):
+                for part in range(2):
+                    result[degree, part, p, rows] = values[2 * degree + part]
+            return inner
+
+        lax.fori_loop(0, block // piece, body, 0)
+        copy(p).start()
+        return carry
+
+    values = factors[...]
+    sub = lax.broadcasted_iota(jnp.int32, values.shape, 0)
+    lane = lax.broadcasted_iota(jnp.int32, values.shape, 1)
+    for part in range(2):
+        pair[part] = jnp.sum(jnp.where((sub == 4 + part) & (lane < nodes), values, 0.0))
+    trace_copy = pltpu.make_async_copy(pair, trace, sems.at[depth])
+    trace_copy.start()
+    lax.fori_loop(0, depth, plane, 0)
+    for p in range(depth):
+        copy(p).wait()
+    trace_copy.wait()
+
+
 def per_device(nodes, slabs, probes, potential, warm_start, shift_points, quad_weights):
     depth, width, length = potential.shape
     block = width // nodes
@@ -845,19 +882,21 @@
     f32, bf16 = jnp.float32, jnp.bfloat16
     anywhere = pl.BlockSpec(memory_space=pltpu.HBM)
     vector = pl.BlockSpec(memory_space=pltpu.VMEM)
-    scalars = pl.BlockSpec(memory_space=pltpu.SMEM)
     dma = pltpu.SemaphoreType.DMA
     small = small_matrices(block, depth)
     picks = halo_picks(width, nodes)
     cpicks = picks if narrow else core_picks(width, nodes)
-    return pl.pallas_call(
+    results = pl.pallas_call(
         functools.partial(kernel, nodes, slabs),
         out_shape=(
             pltpu.VMEM((2, 1, 2, depth, block, length), f32),
-            jax.ShapeDtypeStruct((2,), f32),
+            pltpu.VMEM((nodes, 2, depth + 4, block, length), f32),
+            pltpu.VMEM((nodes, 2, depth + 2, block, length), f32),
+            pltpu.VMEM((nodes, 8, length), f32),
+            pltpu.VMEM((SUMS, 128), f32),
         ),
         in_specs=[anywhere] * 9,
-        out_specs=(vector, scalars),
+        out_specs=(vector,) * 5,
         scratch_shapes=[
             pltpu.VMEM((2, depth, width, length), bf16),
             pltpu.VMEM((nodes, 2, pairs, 16, length), bf16),
@@ -870,11 +909,9 @@
             pltpu.VMEM((2, depth, 8, length), f32),
             pltpu.VMEM((4 * depth, length), f32),
             pltpu.VMEM((4 * depth, length), f32),
-            pltpu.VMEM((nodes, 2, depth + 4, block, length), f32),
             pltpu.VMEM((nodes, 2, 4 * depth, length), f32),
             pltpu.VMEM((nodes, 2, 2, tall, length), bf16),
             pltpu.VMEM((nodes, 2, 2, tall, length), bf16),
-            pltpu.VMEM((nodes, 2, depth + 2, block, length), f32),
             pltpu.VMEM((nodes, 2, 16, length), f32),
             pltpu.VMEM((nodes, 2, 16, length), f32),
             pltpu.VMEM((nodes, 2, 16, length), bf16),
@@ -905,7 +942,7 @@
             dma((nodes * slabs,)),
         ],
         compiler_params=pltpu.CompilerParams(
-            collective_id=0, has_side_effects=True, vmem_limit_bytes=58 * 1024 * 1024
+            collective_id=0, has_side_effects=True, vmem_limit_bytes=48 * 1024 * 1024
         ),
     )(
         warm_start,
@@ -918,6 +955,21 @@
         jnp.asarray(picks),
         jnp.asarray(cpicks),
     )
+    return pl.pallas_call(
+        functools.partial(finish, nodes),
+        out_shape=(
+            jax.ShapeDtypeStruct((2, 1, 2, depth, block, length), f32),
+            jax.ShapeDtypeStruct((2,), f32),
+        ),
+        in_specs=[vector] * 5,
+        out_specs=(anywhere, anywhere),
+        scratch_shapes=[
+            pltpu.VMEM((2, 2, depth, block, length), f32),
+            pltpu.SMEM((2,), f32),
+            dma((depth + 1,)),
+        ],
+        compiler_params=pltpu.CompilerParams(vmem_limit_bytes=4 * 1024 * 1024),
+    )(*results)
 
 
 def solution(mesh):

time: 49.4 us -> 48 us (0.972)
  local copies, waits for them, and re-layouts: 1.53 us -> 0 us
    pallas_call x0 -> x1, Pallas kernels: none -> 2.16 us  [per_device(): pl.pallas_call(functools.partial(finish, nodes), out_shape=(jax.ShapeDtyp...]
    pallas_call x1, Pallas kernels: 47.1 us -> 45 us  [per_device(): pl.pallas_call(functools.partial(kernel, nodes, slabs), out_shape=(pltpu....]
    unnamed x4 -> x0, local copies, waits for them, and re-layouts: 1.53 us -> none
where the time goes in v4:
time: 48 us; the launch traced here: 47.8 us
  Pallas kernels  47.2 us (98%)
  between operations  0.64 us (1%)
    pallas_call x1, Pallas kernels, per_device(): pl.pallas_call(functools.partial(kernel, nodes, slabs), out_shape=(pltpu....  45 us
    pallas_call x1, Pallas kernels, per_device(): pl.pallas_call(functools.partial(finish, nodes), out_shape=(jax.ShapeDtyp...  2.16 us

profile of v4, /device:TPU:0, one launch (start us, length us, event | category | flops | bytes accessed | tf_op | source)
XLA Modules:
  0.0 47.8 jit_solution(1328081837957396924)
XLA Ops:
  0.6 45.0 %shard_map.95 = (f32[2,1,2,6,48,256]{5,4,3,2,1,0:T(8,128)S(1)}, f32[4,2,10,48,256]{4,3,2,1,0:T(8,128)S(1)}, f32[4,2,8,48,256]{4,3,2,1,0:T(8,128)S(1)}, f32[4,8,256]{2,1,0:T(8,128)S(1)}, f32[16,128]{1,0:T(8,128)S(1)}) custom-call(bf16[1,1,2,6,192,256]{5,4,3,2,1,0:T(8,128)(2,1)} %warm.1, f32[1,6,192,256]{3,2,1,0:T(8,128)} %probes.1, f32[6,192,256]{2,1,0:T(8,128)} %potential.1, ...), custom_call_target="tpu_custom_call" | custom-call | tf_op jit(solution)/shard_map/pallas_call | solution.py:889
  45.7 2.2 %shard_map.96 = (f32[2,1,2,6,48,256]{5,4,3,2,1,0:T(8,128)}, f32[2]{0:T(128)}) custom-call(f32[2,1,2,6,48,256]{5,4,3,2,1,0:T(8,128)S(1)} %get-tuple-element.7.started, f32[4,2,10,48,256]{4,3,2,1,0:T(8,128)S(1)} %get-tuple-element.8.rbuf, f32[4,2,8,48,256]{4,3,2,1,0:T(8,128)S(1)} %get-tuple-element.9.qbuf, f32[4,8,256]{2,1,0:T(8,128)S(1)} %get-tuple-element.10.scales, ...), custom_call_target="tpu_custom_call" | custom-call | tf_op jit(solution)/shard_map/pallas_call | solution.py:958

commit v5 on v4

--- a/solution.py
+++ b/solution.py
@@ -374,13 +374,15 @@
                         csend[m, part, p] = picked[tall * m : tall * m + tall]
 
     def send_cores():
+        for c in range(2):
+            forward(0, c).start()
+        for copy in sides:
+            copy.start()
+        for c in range(2, 4):
+            forward(0, c).start()
         for k, c in order:
             if c < 2 or not narrow:
                 gather_copy(k, c).start()
-        for c in range(4):
-            forward(0, c).start()
-        for copy in sides:
-            copy.start()
 
     if narrow:
         send_cores()
@@ -444,7 +446,7 @@
             return carry
 
         zero = jnp.zeros((8, length), f32)
-        for i, total in enumerate(lax.fori_loop(low, high, body, (zero,) * count)):
+        for i, total in enumerate(lax.fori_loop(low, high, body, (zero,) * count, unroll=True)):
             acc[k * SUMS + first + i] += total
 
     def wide(values):
@@ -571,23 +573,20 @@
 
         for c in range(2):
             forward(k, c).wait_recv()
-            forward_halo(k, c).wait_recv()
         added(k, 0, 6, 1, pairs + 1, functools.partial(residual_terms, k))
 
         for c, at in enumerate((3, depth)):
             for part in range(2):
                 far_out[k, c, part] = narrowed(rbuf[k, part, at])
             far_copy(k, c).start()
-        return carry
-
-    def inner_step(k, carry):
+        for c in range(2):
+            forward_halo(k, c).wait_recv()
         edge_rows(k)
         added(k, 6, 6, 1, pairs - 1, functools.partial(image_terms, k))
         return carry
 
     with jax.named_scope("residual"):
         lax.fori_loop(0, nodes, own_step, 0)
-        lax.fori_loop(0, nodes, inner_step, 0)
 
     for copy in sides:
         copy.wait_recv()
@@ -711,7 +710,7 @@
                     moments[degree, 0, part, p, rows] = values[2 * degree + part]
             return carry
 
-        lax.fori_loop(0, block // piece, body, 0)
+        lax.fori_loop(0, block // piece, body, 0, unroll=True)
 
     def start_rows(p, rows):
         values = [None] * 4
@@ -749,15 +748,14 @@
         me = node * slabs + slab
         for row, values in enumerate(spread):
             sums[me, row : row + 1] = jnp.sum(values, axis=0, keepdims=True)
+        hops = [(sum(map(bool, steps[k])), min(b, slabs - b), k, b) for k in range(nodes) for b in range(slabs)]
         scalar_copies = []
-        for a in range(nodes):
-            for b in range(slabs):
-                if a or b:
-                    there = lax.rem(node + a, nodes), lax.rem(slab + b, slabs)
-                    at = a * slabs + b
-                    scalar_copies.append(
-                        remote(sums.at[me], sums.at[me], s_send.at[at], s_recv.at[at], there)
-                    )
+        for _, _, k, b in sorted(hops, reverse=True)[:-1]:
+            at = k * slabs + b
+            there = peer(k), lax.rem(slab + b, slabs)
+            scalar_copies.append(
+                remote(sums.at[me], sums.at[me], s_send.at[at], s_recv.at[at], there)
+            )
         for copy in scalar_copies:
             copy.start()
         lax.fori_loop(0, depth, start_plane, 0)
@@ -856,7 +854,7 @@
                     result[degree, part, p, rows] = values[2 * degree + part]
             return inner
 
-        lax.fori_loop(0, block // piece, body, 0)
+        lax.fori_loop(0, block // piece, body, 0, unroll=True)
         copy(p).start()
         return carry
 
@@ -867,7 +865,7 @@
         pair[part] = jnp.sum(jnp.where((sub == 4 + part) & (lane < nodes), values, 0.0))
     trace_copy = pltpu.make_async_copy(pair, trace, sems.at[depth])
     trace_copy.start()
-    lax.fori_loop(0, depth, plane, 0)
+    lax.fori_loop(0, depth, plane, 0, unroll=2)
     for p in range(depth):
         copy(p).wait()
     trace_copy.wait()

time: 48 us -> 45.4 us (0.946)
  Pallas kernels: 47.2 us -> 44.6 us
    pallas_call x1, Pallas kernels: 45 us -> 42.7 us  [per_device(): pl.pallas_call(functools.partial(kernel, nodes, slabs), out_shape=(pltpu....]
where the time goes in v5:
time: 45.4 us; the launch traced here: 45.3 us
  Pallas kernels  44.6 us (98%)
  between operations  0.64 us (1%)
    pallas_call x1, Pallas kernels, per_device(): pl.pallas_call(functools.partial(kernel, nodes, slabs), out_shape=(pltpu....  42.7 us
    pallas_call x1, Pallas kernels, per_device(): pl.pallas_call(functools.partial(finish, nodes), out_shape=(jax.ShapeDtyp...  1.93 us

profile of v5, /device:TPU:0, one launch (start us, length us, event | category | flops | bytes accessed | tf_op | source)
XLA Modules:
  0.0 45.3 jit_solution(2389291308899097456)
XLA Ops:
  0.6 42.7 %shard_map.95 = (f32[2,1,2,6,48,256]{5,4,3,2,1,0:T(8,128)S(1)}, f32[4,2,10,48,256]{4,3,2,1,0:T(8,128)S(1)}, f32[4,2,8,48,256]{4,3,2,1,0:T(8,128)S(1)}, f32[4,8,256]{2,1,0:T(8,128)S(1)}, f32[16,128]{1,0:T(8,128)S(1)}) custom-call(bf16[1,1,2,6,192,256]{5,4,3,2,1,0:T(8,128)(2,1)} %warm.1, f32[1,6,192,256]{3,2,1,0:T(8,128)} %probes.1, f32[6,192,256]{2,1,0:T(8,128)} %potential.1, ...), custom_call_target="tpu_custom_call" | custom-call | tf_op jit(solution)/shard_map/pallas_call | solution.py:887
  43.3 1.9 %shard_map.96 = (f32[2,1,2,6,48,256]{5,4,3,2,1,0:T(8,128)}, f32[2]{0:T(128)}) custom-call(f32[2,1,2,6,48,256]{5,4,3,2,1,0:T(8,128)S(1)} %get-tuple-element.7.started, f32[4,2,10,48,256]{4,3,2,1,0:T(8,128)S(1)} %get-tuple-element.8.rbuf, f32[4,2,8,48,256]{4,3,2,1,0:T(8,128)S(1)} %get-tuple-element.9.qbuf, f32[4,8,256]{2,1,0:T(8,128)S(1)} %get-tuple-element.10.scales, ...), custom_call_target="tpu_custom_call" | custom-call | tf_op jit(solution)/shard_map/pallas_call | solution.py:956

commit v6 on v5

--- a/solution.py
+++ b/solution.py
@@ -36,9 +36,8 @@
     tall = up_to(block, 16)
     pairs = depth // 2
     sizes = {
-        "own": (tall, tall),
-        "halo0": (tall, 16),
-        "halo1": (tall, 16),
+        "near0": (tall, tall + 16),
+        "near1": (tall, tall + 16),
         "split0": (tall, 2 * block + 16),
         "split1": (tall, 2 * block + 16),
         "ahead": (tall, 2 * block),
@@ -63,8 +62,8 @@
     for i in range(block):
         for j in range(block):
             w = weight_of(i - j)
-            view["own"][i, j] = w
             for s in range(2):
+                view[f"near{s}"][i, j] = w
                 view[f"split{s}"][i, j] = w
                 view[f"split{s}"][i, block + j] = w
             if j > i:
@@ -72,7 +71,7 @@
                 view["ahead"][i, block + j] = 2 * w
         for s in range(2):
             for c, x in enumerate(wide):
-                view[f"halo{s}"][i, 8 * s + c] = weight_of(i - x)
+                view[f"near{s}"][i, tall + 8 * s + c] = weight_of(i - x)
             for c, x in enumerate(slim):
                 view[f"split{s}"][i, 2 * block + 4 * s + c] = weight_of(i - x)
                 view[f"split{s}"][i, 2 * block + 8 + 4 * s + c] = weight_of(i - x)
@@ -457,11 +456,8 @@
         stencil, field = [], []
         for part in range(2):
             centre = wbuf[k, part, pp + 2]
-            plane = (
-                dot(centre, along_y[...])
-                + dot(matrix("own"), centre)
-                + dot(matrix(f"halo{s}"), halo[k, part, i])
-            )[0:block]
+            stacked = jnp.concatenate([centre, halo[k, part, i]], axis=0)
+            plane = (dot(centre, along_y[...]) + dot(matrix(f"near{s}"), stacked))[0:block]
             at = [wide(wbuf[k, part, pp + j]) for j in (0, 1, 3, 4)]
             stencil.append(plane + 16.0 * (at[1] + at[2]) - (at[0] + at[3]))
             field.append(wide(centre))
@@ -692,7 +688,7 @@
 
     with jax.named_scope("energy"):
         lax.fori_loop(0, nodes, energy_step, 0)
-        lax.fori_loop(0, nodes, cross_step, 0)
+        lax.fori_loop(0, nodes, cross_step, 0, unroll=True)
 
     piece = 16 if narrow else block
     factor = []

time: 45.4 us -> 45.2 us (level)
  no operation moved by 1% of the time
where the time goes in v6:
time: 45.2 us; the launch traced here: 45 us
  Pallas kernels  44.4 us (98%)
  between operations  0.64 us (1%)
    pallas_call x1, Pallas kernels, per_device(): pl.pallas_call(functools.partial(kernel, nodes, slabs), out_shape=(pltpu....  42.5 us
    pallas_call x1, Pallas kernels, per_device(): pl.pallas_call(functools.partial(finish, nodes), out_shape=(jax.ShapeDtyp...  1.93 us

profile of v6, /device:TPU:0, one launch (start us, length us, event | category | flops | bytes accessed | tf_op | source)
XLA Modules:
  0.0 45.0 jit_solution(17724957285885684362)
XLA Ops:
  0.6 42.5 %shard_map.95 = (f32[2,1,2,6,48,256]{5,4,3,2,1,0:T(8,128)S(1)}, f32[4,2,10,48,256]{4,3,2,1,0:T(8,128)S(1)}, f32[4,2,8,48,256]{4,3,2,1,0:T(8,128)S(1)}, f32[4,8,256]{2,1,0:T(8,128)S(1)}, f32[16,128]{1,0:T(8,128)S(1)}) custom-call(bf16[1,1,2,6,192,256]{5,4,3,2,1,0:T(8,128)(2,1)} %warm.1, f32[1,6,192,256]{3,2,1,0:T(8,128)} %probes.1, f32[6,192,256]{2,1,0:T(8,128)} %potential.1, ...), custom_call_target="tpu_custom_call" | custom-call | tf_op jit(solution)/shard_map/pallas_call | solution.py:883
  43.1 1.9 %shard_map.96 = (f32[2,1,2,6,48,256]{5,4,3,2,1,0:T(8,128)}, f32[2]{0:T(128)}) custom-call(f32[2,1,2,6,48,256]{5,4,3,2,1,0:T(8,128)S(1)} %get-tuple-element.7.started, f32[4,2,10,48,256]{4,3,2,1,0:T(8,128)S(1)} %get-tuple-element.8.rbuf, f32[4,2,8,48,256]{4,3,2,1,0:T(8,128)S(1)} %get-tuple-element.9.qbuf, f32[4,8,256]{2,1,0:T(8,128)S(1)} %get-tuple-element.10.scales, ...), custom_call_target="tpu_custom_call" | custom-call | tf_op jit(solution)/shard_map/pallas_call | solution.py:952
